TPU v7x, 32 devices: a whole 2x2x4 slice. The times are simulated.
32 devices in a mesh: stream: 4 (over x, core), cross: 8 (over z, y).
Axes of the slice: x: 2, y: 2, z: 4, core: 2. Of those that a mesh axis runs over, the one named last changes fastest.
Arguments:
- residual: bfloat16 [16, 64, 64, 128], P('stream', 'cross'), may hold values from -6 to 6
- approx_inverse: bfloat16 [4, 768, 64, 256], P('stream', 'cross'), may hold values from -0.375 to 0.375
- pattern: int32 [4, 768, 4], P('stream', 'cross'), may hold values from 0 to 95
- live_blocks: int32 [4, 8], P('stream', 'cross'), may hold values from 1 to 32, as said below
- block_aggregate: int32 [16, 64], P('stream', 'cross'), may hold values from 0 to 31
- coarse_inverse: float32 [128, 256], P('stream', 'cross'), may hold values from -0.12 to 0.12
Outputs:
- correction: float32 [16, 64, 64, 128], P('stream', 'cross')
Inputs may be any that keep to these rules, and one draw needn't show every extreme that they name: `pattern`: block numbers of the extended grid, numbered row by row. `live_blocks`: some subdomain is full in every draw.
All inputs are finite; a program needn't handle non-finite values.
Results may differ from a plain program's by a relative error of at most 0.0065.
Values may be sent and summed in bfloat16 or wider, within the bound.
A program may use at most 64 MiB of HBM per device.

v0:
```python
import jax
import jax.numpy as jnp
from jax import lax
from jax.sharding import PartitionSpec as P


def with_halo(cells, sides, width):
    for axis, dim in sides:
        count = lax.axis_size(axis)
        ends = count - 1
        head = lax.slice_in_dim(cells, 0, width, axis=dim)
        tail = lax.slice_in_dim(cells, cells.shape[dim] - width, cells.shape[dim], axis=dim)
        cells = jnp.concatenate(
            [
                lax.ppermute(tail, axis, [(i, (i + 1) % count) for i in range(ends)]),
                cells,
                lax.ppermute(head, axis, [((i + 1) % count, i) for i in range(ends)]),
            ],
            axis=dim,
        )
    return cells


def fold_margin(grid, along, length):
    middle = lax.slice_in_dim(grid, 4, length + 4, axis=along)
    lower = lax.slice_in_dim(grid, 0, 2, axis=along)
    upper = lax.slice_in_dim(grid, length + 6, length + 8, axis=along)
    low_pad = [(0, 0)] * grid.ndim
    high_pad = [(0, 0)] * grid.ndim
    low_pad[along] = (0, length - 2)
    high_pad[along] = (length - 2, 0)
    return middle + jnp.pad(lower, low_pad) + jnp.pad(upper, high_pad)


def body(residual, approx_inverse, pattern, live_blocks, block_aggregate, coarse_inverse):
    rows, columns, width, sides = residual.shape
    local = jnp.arange(rows)[:, None] * columns + jnp.arange(columns)[None, :]
    live = local < live_blocks[0, 0]
    masked = jnp.where(live[:, :, None, None], residual, jnp.zeros((), jnp.bfloat16))
    extent = (rows + 4) * (columns + 4)
    links = pattern[0]
    blocks = approx_inverse[0]
    depth = blocks.shape[2]
    extended = with_halo(masked, (("stream", 0), ("cross", 1)), 2)
    picked = extended.reshape(extent, width, sides)[links].reshape(extent, depth, sides)
    fixes = jnp.einsum("nac,ncr->nar", blocks, picked, preferred_element_type=jnp.float32)
    fixes = fixes.reshape(rows + 4, columns + 4, width, sides).astype(jnp.bfloat16)
    gathered = with_halo(fixes, (("stream", 0), ("cross", 1)), 2).astype(jnp.float32)
    fine = fold_margin(fold_margin(gathered, 0, rows), 1, columns)
    cells = width // 4
    per_block = masked.reshape(rows, columns, 4, cells, sides).astype(jnp.float32).sum(axis=3)
    per_block = per_block.reshape(rows * columns, 4 * sides)
    owned = coarse_inverse.shape[0] // 4
    groups = owned * lax.axis_size("stream")
    onehot = (
        block_aggregate.reshape(-1)[:, None] == jnp.arange(groups, dtype=jnp.int32)[None, :]
    ).astype(jnp.float32)
    chosen = onehot
    owned_sums = lax.psum_scatter(
        jnp.dot(chosen.T, per_block, precision=lax.Precision.HIGHEST).astype(jnp.bfloat16),
        "stream",
        scatter_dimension=0,
        tiled=True,
    ).astype(jnp.float32)
    coarse = jnp.dot(
        coarse_inverse, owned_sums.reshape(owned * 4, sides), precision=lax.Precision.HIGHEST
    )
    coarse = coarse.reshape(owned, 4 * sides)
    chosen = onehot
    prolonged = jnp.dot(
        chosen,
        lax.all_gather(coarse, "stream", axis=0, tiled=True),
        precision=lax.Precision.HIGHEST,
    )
    spread = jnp.broadcast_to(
        prolonged.reshape(rows, columns, 4, 1, sides), (rows, columns, 4, cells, sides)
    )
    spread = spread.reshape(rows, columns, width, sides)
    return jnp.where(live[:, :, None, None], fine + spread, jnp.zeros((), jnp.float32))


def solution(mesh):
    placed = (
        P("stream", "cross", None, None),
        P("stream", "cross", None, None),
        P("stream", "cross", None),
        P("stream", "cross"),
        P("stream", "cross"),
        P("stream", "cross"),
    )
    return jax.shard_map(
        body,
        mesh=mesh,
        in_specs=placed,
        out_specs=P("stream", "cross", None, None),
        check_vma=False,
    )
```

profile of v0, /device:TPU:17, one launch (start us, length us, event | category | flops | bytes accessed | tf_op | source)
XLA Modules:
  0.0 96.3 jit_solution(1834988471570388678)
XLA Ops:
  7.4 2.1 %convert_reduce_fusion = (f32[4,8,4,128]{3,2,1,0:T(4,128)}, bf16[4,8,64,128]{3,2,1,0:T(8,128)(2,1)S(1)}) fusion(bf16[4,8,64,128]{3,2,1,0:T(8,128)(2,1)} %param.6, pred[4,8]{1,0:T(4,128)(4,1)S(1)} %add_compare_fusion), kind=kLoop, calls=%fused_computation.17 | loop fusion | flops 770048 | bytes 1114144 | tf_op jit(solution)/shard_map/reduce_sum | solution.py:51
  9.5 3.7 %collective-permute-start = (bf16[2,8,64,128]{3,2,1,0:T(8,128)(2,1)S(1)}, bf16[2,8,64,128]{3,2,1,0:T(8,128)(2,1)S(1)}, u32[]{:S(2)}, u32[]{:S(2)}) collective-permute-start(bf16[2,8,64,128]{3,2,1,0:T(8,128)(2,1)S(1)} %get-tuple-element.13), channel_id=1, source_target_pairs={{0,8},{8,16},{16,24},{1,9},{9,17},{17,25},{2,10},{10,18},{18,26},{... | collective-permute-start | bytes 786440 | tf_op jit(solution)/shard_map/ppermute | solution.py:15
  13.2 1.9 %collective-permute-start.1 = (bf16[2,8,64,128]{3,2,1,0:T(8,128)(2,1)S(1)}, bf16[2,8,64,128]{3,2,1,0:T(8,128)(2,1)S(1)}, u32[]{:S(2)}, u32[]{:S(2)}) collective-permute-start(bf16[2,8,64,128]{3,2,1,0:T(8,128)(2,1)S(1)} %get-tuple-element.14), channel_id=1, source_target_pairs={{8,0},{16,8},{24,16},{9,1},{17,9},{25,17},{10,2},{18,10},{26,18},{... | collective-permute-start | bytes 786440 | tf_op jit(solution)/shard_map/ppermute | solution.py:17
  15.2 1.4 %collective-permute-done = bf16[2,8,64,128]{3,2,1,0:T(8,128)(2,1)S(1)} collective-permute-done((bf16[2,8,64,128]{3,2,1,0:T(8,128)(2,1)S(1)}, bf16[2,8,64,128]{3,2,1,0:T(8,128)(2,1)S(1)}, u32[]{:S(2)}, u32[]{:S(2)}) %collective-permute-start) | collective-permute-done | bytes 262176 | tf_op jit(solution)/shard_map/ppermute | solution.py:15
  16.5 4.4 %collective-permute-done.1 = bf16[2,8,64,128]{3,2,1,0:T(8,128)(2,1)S(1)} collective-permute-done((bf16[2,8,64,128]{3,2,1,0:T(8,128)(2,1)S(1)}, bf16[2,8,64,128]{3,2,1,0:T(8,128)(2,1)S(1)}, u32[]{:S(2)}, u32[]{:S(2)}) %collective-permute-start.1) | collective-permute-done | bytes 262176 | tf_op jit(solution)/shard_map/ppermute | solution.py:17
  21.8 3.1 %collective-permute-start.2 = (bf16[8,2,64,128]{3,2,1,0:T(8,128)(2,1)}, bf16[8,2,64,128]{3,2,1,0:T(8,128)(2,1)}, u32[]{:S(2)}, u32[]{:S(2)}) collective-permute-start(bf16[8,2,64,128]{3,2,1,0:T(8,128)(2,1)} %get-tuple-element.11), channel_id=1, source_target_pairs={{0,1},{1,2},{2,3},{3,4},{4,5},{5,6},{6,7},{8,9},{9,10},{10,11},{11... | collective-permute-start | bytes 786440 | tf_op jit(solution)/shard_map/ppermute | solution.py:15
  25.0 3.0 %collective-permute-start.3 = (bf16[8,2,64,128]{3,2,1,0:T(8,128)(2,1)}, bf16[8,2,64,128]{3,2,1,0:T(8,128)(2,1)}, u32[]{:S(2)}, u32[]{:S(2)}) collective-permute-start(bf16[8,2,64,128]{3,2,1,0:T(8,128)(2,1)} %get-tuple-element.12), channel_id=1, source_target_pairs={{1,0},{2,1},{3,2},{4,3},{5,4},{6,5},{7,6},{9,8},{10,9},{11,10},{12... | collective-permute-start | bytes 786440 | tf_op jit(solution)/shard_map/ppermute | solution.py:17
  28.3 5.9 %collective-permute-done.2 = bf16[8,2,64,128]{3,2,1,0:T(8,128)(2,1)} collective-permute-done((bf16[8,2,64,128]{3,2,1,0:T(8,128)(2,1)}, bf16[8,2,64,128]{3,2,1,0:T(8,128)(2,1)}, u32[]{:S(2)}, u32[]{:S(2)}) %collective-permute-start.2) | collective-permute-done | bytes 262176 | tf_op jit(solution)/shard_map/ppermute | solution.py:15
  34.8 2.7 %pad_maximum_fusion = bf16[8,12,64,128]{3,2,1,0:T(8,128)(2,1)} fusion(bf16[8,2,64,128]{3,2,1,0:T(8,128)(2,1)} %collective-permute-done.3, bf16[2,8,64,128]{3,2,1,0:T(8,128)(2,1)} %copy-done.4, bf16[4,8,64,128]{3,2,1,0:T(8,128)(2,1)} %copy-done.3, bf16[2,8,64,128]{3,2,1,0:T(8,128)(2,1)S(1)} %collective-permute-done, ...), kind=kLoop, calls=%fused_computation.8 | loop fusion | flops 3145728 | bytes 3145728 | tf_op jit(solution)/shard_map/concatenate | solution.py:13
  37.5 5.4 %gather_fusion = bf16[384,64,128]{2,1,0:T(8,128)(2,1)} fusion(bf16[96,64,128]{2,1,0:T(8,128)(2,1)} %bitcast.36, s32[1024]{0:T(1024)S(1)} %pad_clamp_fusion), kind=kCustom, calls=%fused_computation | custom fusion | bytes 12584448 | tf_op jit(solution)/shard_map/gather | solution.py:45
  42.9 4.0 %fusion.4 = bf16[96,128,64]{1,2,0:T(8,128)(2,1)S(1)} fusion(bf16[96,256,128]{2,1,0:T(8,128)(2,1)} %bitcast.41, bf16[1,96,64,256]{3,2,1,0:T(8,128)(2,1)S(1)} %copy-done), kind=kOutput, calls=%fused_computation.7 | convolution fusion | flops 403439616 | bytes 11010048 | tf_op jit(solution)/shard_map/nac,ncr->nar/dot_general | solution.py:46
  49.0 1.9 %collective-permute-start.5 = (bf16[2,12,64,128]{3,2,1,0:T(8,128)(2,1)}, bf16[2,12,64,128]{3,2,1,0:T(8,128)(2,1)S(1)}, u32[]{:S(2)}, u32[]{:S(2)}) collective-permute-start(bf16[2,12,64,128]{3,2,1,0:T(8,128)(2,1)} %bitcast.8), channel_id=1, source_target_pairs={{8,0},{16,8},{24,16},{9,1},{17,9},{25,17},{10,2},{18,10},{26,18},{... | collective-permute-start | bytes 1179656 | tf_op jit(solution)/shard_map/ppermute | solution.py:17
  50.9 3.6 %collective-permute-start.4 = (bf16[2,12,64,128]{3,2,1,0:T(8,128)(2,1)}, bf16[2,12,64,128]{3,2,1,0:T(8,128)(2,1)}, u32[]{:S(2)}, u32[]{:S(2)}) collective-permute-start(bf16[2,12,64,128]{3,2,1,0:T(8,128)(2,1)} %bitcast.6), channel_id=1, source_target_pairs={{0,8},{8,16},{16,24},{1,9},{9,17},{17,25},{2,10},{10,18},{18,26},{... | collective-permute-start | bytes 1179656 | tf_op jit(solution)/shard_map/ppermute | solution.py:15
  54.7 1.7 %convolution_convert_fusion = bf16[32,512]{1,0:T(8,128)(2,1)} fusion(f32[4,8,4,128]{3,2,1,0:T(4,128)} %get-tuple-element.5, s32[32]{0:T(128)S(1)} %eq.15), kind=kOutput, calls=%fused_computation.10 | convolution fusion | flops 6308864 | bytes 98432 | tf_op jit(solution)/shard_map/dot_general | solution.py:60
  56.4 1.9 %collective-permute-done.5 = bf16[2,12,64,128]{3,2,1,0:T(8,128)(2,1)S(1)} collective-permute-done((bf16[2,12,64,128]{3,2,1,0:T(8,128)(2,1)}, bf16[2,12,64,128]{3,2,1,0:T(8,128)(2,1)S(1)}, u32[]{:S(2)}, u32[]{:S(2)}) %collective-permute-start.5) | collective-permute-done | bytes 393248 | tf_op jit(solution)/shard_map/ppermute | solution.py:17
  58.3 1.3 %collective-permute-done.4 = bf16[2,12,64,128]{3,2,1,0:T(8,128)(2,1)} collective-permute-done((bf16[2,12,64,128]{3,2,1,0:T(8,128)(2,1)}, bf16[2,12,64,128]{3,2,1,0:T(8,128)(2,1)}, u32[]{:S(2)}, u32[]{:S(2)}) %collective-permute-start.4) | collective-permute-done | bytes 393248 | tf_op jit(solution)/shard_map/ppermute | solution.py:15
  59.6 2.0 %pad_maximum_fusion.3 = (bf16[12,2,64,128]{3,2,1,0:T(8,128)(2,1)}, bf16[12,2,64,128]{3,2,1,0:T(8,128)(2,1)}) fusion(bf16[2,12,64,128]{3,2,1,0:T(8,128)(2,1)S(1)} %collective-permute-done.5, bf16[8,12,64,128]{3,2,1,0:T(8,128)(2,1)} %bitcast.38, bf16[2,12,64,128]{3,2,1,0:T(8,128)(2,1)} %collective-permute-done.4), kind=kLoop, calls=%fused_computation.22 | loop fusion | flops 786432 | bytes 3145728 | tf_op jit(solution)/shard_map/slice | solution.py:12
  61.6 3.2 %collective-permute-start.6 = (bf16[12,2,64,128]{3,2,1,0:T(8,128)(2,1)}, bf16[12,2,64,128]{3,2,1,0:T(8,128)(2,1)}, u32[]{:S(2)}, u32[]{:S(2)}) collective-permute-start(bf16[12,2,64,128]{3,2,1,0:T(8,128)(2,1)} %get-tuple-element.7), channel_id=1, source_target_pairs={{0,1},{1,2},{2,3},{3,4},{4,5},{5,6},{6,7},{8,9},{9,10},{10,11},{11... | collective-permute-start | bytes 1179656 | tf_op jit(solution)/shard_map/ppermute | solution.py:15
  64.8 2.9 %collective-permute-start.7 = (bf16[12,2,64,128]{3,2,1,0:T(8,128)(2,1)}, bf16[12,2,64,128]{3,2,1,0:T(8,128)(2,1)}, u32[]{:S(2)}, u32[]{:S(2)}) collective-permute-start(bf16[12,2,64,128]{3,2,1,0:T(8,128)(2,1)} %get-tuple-element.8), channel_id=1, source_target_pairs={{1,0},{2,1},{3,2},{4,3},{5,4},{6,5},{7,6},{9,8},{10,9},{11,10},{12... | collective-permute-start | bytes 1179656 | tf_op jit(solution)/shard_map/ppermute | solution.py:17
  67.8 6.7 %reduce-scatter.2.cloned.1.call-done = bf16[8,512]{1,0:T(8,128)(2,1)} async-done(((bf16[32,512]{1,0:T(8,128)(2,1)}), bf16[8,512]{1,0:T(8,128)(2,1)}) %reduce-scatter.2.cloned.1.call-update) | async-done | bytes 8208 | tf_op jit(solution)/shard_map/reduce_scatter | solution.py:59
  75.2 1.5 %convolution_bitcast_fusion.1 = f32[32,128]{1,0:T(8,128)} fusion(bf16[32,128]{1,0:T(8,128)(2,1)S(1)} %reshape.85, f32[32,32]{1,0:T(8,128)} %param.11), kind=kOutput, calls=%fused_computation.11 | convolution fusion | flops 1572864 | bytes 28672 | tf_op jit(solution)/shard_map/dot_general | solution.py:65
  77.4 5.9 %all_gather.3 = f32[32,512]{1,0:T(8,128)S(1)} all-gather(f32[8,512]{1,0:T(8,128)S(1)} %reshape.86), channel_id=1, replica_groups=mesh['stream'=4,'cross'=8] {'stream'}, dimensions={0}, use_global_device_ids=true | all-gather | bytes 81920 | tf_op jit(solution)/shard_map/all_gather | solution.py:72
  85.6 1.8 %maximum_convert_fusion = f32[12,16,64,128]{3,2,1,0:T(8,128)S(1)} fusion(bf16[12,2,64,128]{3,2,1,0:T(8,128)(2,1)} %collective-permute-done.7, bf16[2,12,64,128]{3,2,1,0:T(8,128)(2,1)S(1)} %collective-permute-done.5, bf16[8,12,64,128]{3,2,1,0:T(8,128)(2,1)S(1)} %bitcast.40, bf16[2,12,64,128]{3,2,1,0:T(8,128)(2,1)} %collective-permute-done.4, ...), kind=kLoop, calls=%fused_computation.1 | loop fusion | flops 7864320 | bytes 9437184 | tf_op jit(solution)/shard_map/convert_element_type | solution.py:48
  88.2 1.2 %fusion.10 = f32[4,8,64,128]{3,2,1,0:T(8,128)} fusion(f32[4,16,64,128]{3,2,1,0:T(8,128)S(1)} %fusion.3, f32[4,2,64,128]{3,2,1,0:T(8,128)S(1)} %slice.76, f32[4,8,4,128]{3,2,1,0:T(4,128)S(1)} %copy.9, pred[8]{0:T(512)(128)(4,1)S(1)} %copy-done.10, pred[4,8]{1,0:T(4,128)(4,1)S(1)} %copy-done.7), kind=kLoop, calls=%fused_computation.16 | loop fusion | flops 1310720 | bytes 3473448 | tf_op jit(solution)/shard_map/jit(_where)/select_n | solution.py:79
  (46 shorter events, 8.5 us)
Async XLA Ops:
  6.5 36.4 %copy-start = (bf16[1,96,64,256]{3,2,1,0:T(8,128)(2,1)S(1)}, bf16[1,96,64,256]{3,2,1,0:T(8,128)(2,1)}, u32[]{:S(2)}) copy-start(bf16[1,96,64,256]{3,2,1,0:T(8,128)(2,1)} %param.7) | copy-start | bytes 9437188
  6.5 21.5 %copy-start.9 = (s32[1,96,4]{1,2,0:T(4,128)S(1)}, s32[1,96,4]{1,2,0:T(4,128)}, u32[]{:S(2)}) copy-start(s32[1,96,4]{1,2,0:T(4,128)} %param.8) | copy-start | bytes 4612
  6.5 67.9 %reduce-scatter.2.cloned.1.call-start = ((), (), s32[]{:S(2)}) async-start(), calls=%async_computation.1 | async-start | bytes 40960 | tf_op jit(solution)/shard_map/reduce_scatter | solution.py:59
  7.4 5.8 %copy-start.6 = (pred[4,8]{1,0:T(4,128)(4,1)}, pred[4,8]{1,0:T(4,128)(4,1)S(1)}, u32[]{:S(2)}) copy-start(pred[4,8]{1,0:T(4,128)(4,1)S(1)} %add_compare_fusion) | copy-start | bytes 100
  9.5 11.4 %copy-start.3 = (bf16[4,8,64,128]{3,2,1,0:T(8,128)(2,1)}, bf16[4,8,64,128]{3,2,1,0:T(8,128)(2,1)S(1)}, u32[]{:S(2)}) copy-start(bf16[4,8,64,128]{3,2,1,0:T(8,128)(2,1)S(1)} %get-tuple-element.6) | copy-start | bytes 1572868
  9.5 7.0 %collective-permute-start = (bf16[2,8,64,128]{3,2,1,0:T(8,128)(2,1)S(1)}, bf16[2,8,64,128]{3,2,1,0:T(8,128)(2,1)S(1)}, u32[]{:S(2)}, u32[]{:S(2)}) collective-permute-start(bf16[2,8,64,128]{3,2,1,0:T(8,128)(2,1)S(1)} %get-tuple-element.13), channel_id=1, source_target_pairs={{0,8},{8,16},{16,24},{1,9},{9,17},{17,25},{2,10},{10,18},{18,26},{... | collective-permute-start | bytes 786440 | tf_op jit(solution)/shard_map/ppermute | solution.py:15
  13.2 7.7 %collective-permute-start.1 = (bf16[2,8,64,128]{3,2,1,0:T(8,128)(2,1)S(1)}, bf16[2,8,64,128]{3,2,1,0:T(8,128)(2,1)S(1)}, u32[]{:S(2)}, u32[]{:S(2)}) collective-permute-start(bf16[2,8,64,128]{3,2,1,0:T(8,128)(2,1)S(1)} %get-tuple-element.14), channel_id=1, source_target_pairs={{8,0},{16,8},{24,16},{9,1},{17,9},{25,17},{10,2},{18,10},{26,18},{... | collective-permute-start | bytes 786440 | tf_op jit(solution)/shard_map/ppermute | solution.py:17
  20.9 0.9 copy-start.4
  21.8 12.4 %collective-permute-start.2 = (bf16[8,2,64,128]{3,2,1,0:T(8,128)(2,1)}, bf16[8,2,64,128]{3,2,1,0:T(8,128)(2,1)}, u32[]{:S(2)}, u32[]{:S(2)}) collective-permute-start(bf16[8,2,64,128]{3,2,1,0:T(8,128)(2,1)} %get-tuple-element.11), channel_id=1, source_target_pairs={{0,1},{1,2},{2,3},{3,4},{4,5},{5,6},{6,7},{8,9},{9,10},{10,11},{11... | collective-permute-start | bytes 786440 | tf_op jit(solution)/shard_map/ppermute | solution.py:15
  25.0 9.8 %collective-permute-start.3 = (bf16[8,2,64,128]{3,2,1,0:T(8,128)(2,1)}, bf16[8,2,64,128]{3,2,1,0:T(8,128)(2,1)}, u32[]{:S(2)}, u32[]{:S(2)}) collective-permute-start(bf16[8,2,64,128]{3,2,1,0:T(8,128)(2,1)} %get-tuple-element.12), channel_id=1, source_target_pairs={{1,0},{2,1},{3,2},{4,3},{5,4},{6,5},{7,6},{9,8},{10,9},{11,10},{12... | collective-permute-start | bytes 786440 | tf_op jit(solution)/shard_map/ppermute | solution.py:17
  42.9 11.7 %copy-start.8 = (s32[4,8]{1,0:T(4,128)S(1)}, s32[4,8]{1,0:T(4,128)}, u32[]{:S(2)}) copy-start(s32[4,8]{1,0:T(4,128)} %param.10) | copy-start | bytes 388
  46.9 1.2 %copy-start.1 = (bf16[96,128,64]{1,2,0:T(8,128)(2,1)}, bf16[96,128,64]{1,2,0:T(8,128)(2,1)S(1)}, u32[]{:S(2)}) copy-start(bf16[96,128,64]{1,2,0:T(8,128)(2,1)S(1)} %fusion.4) | copy-start | bytes 4718596
  49.0 9.3 %collective-permute-start.5 = (bf16[2,12,64,128]{3,2,1,0:T(8,128)(2,1)}, bf16[2,12,64,128]{3,2,1,0:T(8,128)(2,1)S(1)}, u32[]{:S(2)}, u32[]{:S(2)}) collective-permute-start(bf16[2,12,64,128]{3,2,1,0:T(8,128)(2,1)} %bitcast.8), channel_id=1, source_target_pairs={{8,0},{16,8},{24,16},{9,1},{17,9},{25,17},{10,2},{18,10},{26,18},{... | collective-permute-start | bytes 1179656 | tf_op jit(solution)/shard_map/ppermute | solution.py:17
  50.9 8.7 %collective-permute-start.4 = (bf16[2,12,64,128]{3,2,1,0:T(8,128)(2,1)}, bf16[2,12,64,128]{3,2,1,0:T(8,128)(2,1)}, u32[]{:S(2)}, u32[]{:S(2)}) collective-permute-start(bf16[2,12,64,128]{3,2,1,0:T(8,128)(2,1)} %bitcast.6), channel_id=1, source_target_pairs={{0,8},{8,16},{16,24},{1,9},{9,17},{17,25},{2,10},{10,18},{18,26},{... | collective-permute-start | bytes 1179656 | tf_op jit(solution)/shard_map/ppermute | solution.py:15
  54.7 13.1 %copy-start.5 = (s32[32]{0:T(128)}, s32[32]{0:T(128)S(1)}, u32[]{:S(2)}) copy-start(s32[32]{0:T(128)S(1)} %eq.15) | copy-start | bytes 388
  61.6 22.5 %collective-permute-start.6 = (bf16[12,2,64,128]{3,2,1,0:T(8,128)(2,1)}, bf16[12,2,64,128]{3,2,1,0:T(8,128)(2,1)}, u32[]{:S(2)}, u32[]{:S(2)}) collective-permute-start(bf16[12,2,64,128]{3,2,1,0:T(8,128)(2,1)} %get-tuple-element.7), channel_id=1, source_target_pairs={{0,1},{1,2},{2,3},{3,4},{4,5},{5,6},{6,7},{8,9},{9,10},{10,11},{11... | collective-permute-start | bytes 1179656 | tf_op jit(solution)/shard_map/ppermute | solution.py:15
  64.8 19.3 %collective-permute-start.7 = (bf16[12,2,64,128]{3,2,1,0:T(8,128)(2,1)}, bf16[12,2,64,128]{3,2,1,0:T(8,128)(2,1)}, u32[]{:S(2)}, u32[]{:S(2)}) collective-permute-start(bf16[12,2,64,128]{3,2,1,0:T(8,128)(2,1)} %get-tuple-element.8), channel_id=1, source_target_pairs={{1,0},{2,1},{3,2},{4,3},{5,4},{6,5},{7,6},{9,8},{10,9},{11,10},{12... | collective-permute-start | bytes 1179656 | tf_op jit(solution)/shard_map/ppermute | solution.py:17
  84.1 1.5 %copy-start.2 = (bf16[96,128,64]{1,2,0:T(8,128)(2,1)S(1)}, bf16[96,128,64]{1,2,0:T(8,128)(2,1)}, u32[]{:S(2)}) copy-start(bf16[96,128,64]{1,2,0:T(8,128)(2,1)} %copy-done.1) | copy-start | bytes 4718596
  85.6 1.8 %copy-start.11 = (pred[4]{0:T(512)(128)(4,1)S(1)}, pred[4]{0:T(512)(128)(4,1)}, u32[]{:S(2)}) copy-start(pred[4]{0:T(512)(128)(4,1)} %constant.13.clone.1) | copy-start | bytes 16
  87.4 0.8 copy-start.7
  87.4 0.8 copy-start.10
Sparse Core Ops, SparseCore 0:
  56.6 17.8 reduce-scatter.1
where the time goes:
time: 98.1 us; the launch traced here: 96.3 us
  starting transfers between devices  23.5 us (24%)
  waiting for transfers between devices  22.1 us (23%)
  between operations  14.5 us (15%)
  other arithmetic  12.6 us (13%)
  local copies, waits for them, and re-layouts  9.72 us (10%)
  matrix products  7.99 us (8%)
  blocking collectives  5.92 us (6%)
    ppermute x4, starting transfers between devices, with_halo(): lax.ppermute(tail, axis, [(i, (i + 1) % count) for i in range(ends)])  13.7 us
    ppermute x4, starting transfers between devices, with_halo(): lax.ppermute(head, axis, [((i + 1) % count, i) for i in range(ends)])  9.81 us
    ppermute x4, waiting for transfers between devices, with_halo(): lax.ppermute(tail, axis, [(i, (i + 1) % count) for i in range(ends)])  8.59 us
    ppermute x4, waiting for transfers between devices, with_halo(): lax.ppermute(head, axis, [((i + 1) % count, i) for i in range(ends)])  6.86 us
    reduce_scatter x1, waiting for transfers between devices, body(): lax.psum_scatter(jnp.dot(chosen.T, per_block, precision=lax.Precision.HIG...  6.66 us
    all_gather x1, blocking collectives, body(): lax.all_gather(coarse, 'stream', axis=0, tiled=True)  5.92 us
    gather x1, local copies, waits for them, and re-layouts, body(): extended.reshape(extent, width, sides)[links].reshape(extent, depth, sides)  5.43 us
    dot_general x1, matrix products, body(): jnp.einsum('nac,ncr->nar', blocks, picked, preferred_element_type=jnp.flo...  4.02 us
  transfers between devices with their start and end apart: 9, of which 7 were waited for; matrix products, arithmetic and copies ran while one was open for 8% of the time, Pallas kernels for 0%

commit v1 on v0

v1 whole, which is shorter than its diff:
```python
import functools

import jax
import jax.numpy as jnp
from jax import lax
from jax.experimental import pallas as pl
from jax.experimental.pallas import tpu as pltpu
from jax.sharding import PartitionSpec as P

W = 2


def kernel(
    ns, nc, R, C,
    residual, inverse, pattern, live_ref, aggregate, coarse_inv,
    out,
    res, a_mat, ext4, fix4, rs, rc, msum, pb, partial, part_in, coarse_all,
    in_sem, h_send, h_recv, q_send, q_recv, p_send, p_recv, g_send, g_recv,
    b_send, b_recv, d_send, d_recv,
):
    s = lax.axis_index("stream")
    c = lax.axis_index("cross")
    width, sides = res.shape[2], res.shape[3]
    CE = C + 2 * W
    RE = R + 2 * W
    owned = coarse_inv.shape[0] // 4
    bf16, f32 = jnp.bfloat16, jnp.float32

    s_has = (s > 0, s < ns - 1)
    c_has = (c > 0, c < nc - 1)
    s_to = (jnp.maximum(s - 1, 0), jnp.minimum(s + 1, ns - 1))
    c_to = (jnp.maximum(c - 1, 0), jnp.minimum(c + 1, nc - 1))

    load_res = pltpu.make_async_copy(residual, res, in_sem.at[0])
    load_a = pltpu.make_async_copy(inverse.at[0], a_mat, in_sem.at[1])
    load_res.start()
    load_a.start()

    barrier = pltpu.get_barrier_semaphore()
    for k in range(1, ns):
        pl.semaphore_signal(barrier, inc=1, device_id={"stream": lax.rem(s + k, ns)},
                            device_id_type=pl.DeviceIdType.MESH)
    for e in range(2):
        @pl.when(c_has[e])
        def _():
            pl.semaphore_signal(barrier, inc=1, device_id={"cross": c_to[e]},
                                device_id_type=pl.DeviceIdType.MESH)

    def zero(ref, rows, cols):
        ref[rows[0]:rows[1], cols[0]:cols[1]] = jnp.zeros(
            (rows[1] - rows[0], cols[1] - cols[0], width, sides), bf16)

    @pl.when(s == 0)
    def _():
        zero(ext4, (0, W), (0, CE))
        zero(rs, (0, W), (0, CE))

    @pl.when(s == ns - 1)
    def _():
        zero(ext4, (R + W, RE), (0, CE))
        zero(rs, (W, 2 * W), (0, CE))

    @pl.when(c == 0)
    def _():
        zero(ext4, (0, RE), (0, W))
        zero(rc, (0, R), (0, W))

    @pl.when(c == nc - 1)
    def _():
        zero(ext4, (0, RE), (C + W, CE))
        zero(rc, (0, R), (W, 2 * W))

    live = live_ref[0, 0]
    load_res.wait()

    def mask_row(i, carry):
        for j in range(C):
            block = res[i, j]
            keep = jnp.full(block.shape, i * C + j, jnp.int32) < live
            ext4[i + W, j + W] = jnp.where(keep, block.astype(f32), 0.0).astype(bf16)
        return carry

    lax.fori_loop(0, R, mask_row, 0, unroll=True)

    own_rows = (pl.ds(W, W), pl.ds(R, W))
    halo_rows = (pl.ds(R + W, W), pl.ds(0, W))
    own_cols = (pl.ds(W, W), pl.ds(C, W))
    halo_cols = (pl.ds(C + W, W), pl.ds(0, W))
    side_cols = (pl.ds(0, W), pl.ds(C + W, W))
    mid_rows, mid_cols = pl.ds(W, R), pl.ds(W, C)

    def remote(src, dst, send, recv, to):
        return pltpu.make_async_remote_copy(
            src_ref=src, dst_ref=dst, send_sem=send, recv_sem=recv,
            device_id=to, device_id_type=pl.DeviceIdType.MESH)

    def cross1(e):
        return remote(ext4.at[mid_rows, own_cols[e]], ext4.at[mid_rows, halo_cols[e]],
                      h_send.at[e], h_recv.at[e], {"cross": c_to[e]})

    def stream1(d):
        return remote(ext4.at[own_rows[d], mid_cols], ext4.at[halo_rows[d], mid_cols],
                      h_send.at[2 + d], h_recv.at[2 + d], {"stream": s_to[d]})

    def corner1(d, e):
        return remote(ext4.at[own_rows[d], side_cols[e]], ext4.at[halo_rows[d], side_cols[e]],
                      q_send.at[2 * d + e], q_recv.at[2 * d + e], {"stream": s_to[d]})

    far_rows = (pl.ds(0, W), pl.ds(R + W, W))
    land_rows = (pl.ds(W, W), pl.ds(0, W))

    def corner2(d, e):
        return remote(fix4.at[far_rows[d], side_cols[e]], rs.at[land_rows[d], side_cols[e]],
                      b_send.at[2 * d + e], b_recv.at[2 * d + e], {"stream": s_to[d]})

    def stream2(d):
        return remote(fix4.at[far_rows[d], mid_cols], rs.at[land_rows[d], mid_cols],
                      d_send.at[2 + d], d_recv.at[2 + d], {"stream": s_to[d]})

    def cross2(e):
        return remote(msum.at[:, pl.ds(W * e, W)], rc.at[:, pl.ds(W * (1 - e), W)],
                      d_send.at[e], d_recv.at[e], {"cross": c_to[e]})

    def when(cond, run):
        pl.when(cond)(run)

    pl.semaphore_wait(barrier, ns - 1 + c_has[0].astype(jnp.int32) + c_has[1].astype(jnp.int32))

    for e in range(2):
        when(c_has[e], lambda: cross1(e).start())
    for d in range(2):
        when(s_has[d], lambda: stream1(d).start())

    def sums(m, carry):
        i = m // (C // 2)
        j = (m % (C // 2)) * 2
        rows = []
        for t in range(2):
            block = ext4[i + W, j + W + t].astype(f32)
            rows.append(block.reshape(4, width // 4, sides).sum(axis=1))
        pb[pl.ds(pl.multiple_of(m * 8, 8), 8), :] = jnp.concatenate(rows, axis=0)
        return carry

    lax.fori_loop(0, R * C // 2, sums, 0, unroll=True)
    n_own = R * C
    lane = lax.broadcasted_iota(jnp.int32, (8, 4 * n_own), 1)
    key = jnp.zeros((8, 4 * n_own), jnp.int32)
    for i in range(R):
        for j in range(C):
            key = jnp.where(lane // 4 == i * C + j, aggregate[i, j], key)
    key = (key * 4 + lane % 4)[0:1]
    for o in range(ns):
        row = lax.broadcasted_iota(jnp.int32, (4 * owned, 4 * n_own), 0) + o * 4 * owned
        chosen = (row == jnp.broadcast_to(key, row.shape)).astype(f32)
        partial[o] = jnp.dot(chosen, pb[...], precision=lax.Precision.HIGHEST,
                             preferred_element_type=f32)

    def give(k):
        to = lax.rem(s + k, ns)
        return remote(partial.at[to], part_in.at[k - 1], p_send.at[k - 1], p_recv.at[k - 1],
                      {"stream": to})

    def share(k, mine):
        part = coarse_all.at[pl.ds(mine * owned, owned)]
        return remote(part, part, g_send.at[k - 1], g_recv.at[k - 1],
                      {"stream": lax.rem(s + k, ns)})

    for k in range(1, ns):
        give(k).start()

    for e in range(2):
        when(c_has[1 - e], lambda: cross1(e).wait_recv())
    for d in range(2):
        for e in range(2):
            when(s_has[d] & c_has[e], lambda: corner1(d, e).start())

    total = partial[s]
    for k in range(1, ns):
        give(k).wait_recv()
        total = total + part_in[k - 1]
    coarse = jnp.dot(coarse_inv[...], total, precision=lax.Precision.HIGHEST,
                     preferred_element_type=f32)
    for a in range(owned):
        coarse_all[s * owned + a] = coarse[4 * a:4 * a + 4]
    for k in range(1, ns):
        share(k, s).start()

    load_a.wait()
    for d in range(2):
        when(s_has[1 - d], lambda: stream1(d).wait_recv())
    for d in range(2):
        for e in range(2):
            when(s_has[1 - d] & c_has[e], lambda: corner1(d, e).wait_recv())

    ext = ext4.reshape(RE * CE, width, sides)

    def fix_of(i, j):
        n = i * CE + j
        picked = jnp.concatenate(
            [ext[pattern[0, n, k]] for k in range(a_mat.shape[2] // width)], axis=0)
        return jnp.dot(a_mat[n], picked, preferred_element_type=f32)

    edge = tuple(range(W)) + tuple(range(C + W, CE))

    def sweep(row_of, cols):
        def one(t, carry):
            i = row_of(t)
            for j in cols:
                fix4[i, j] = fix_of(i, j).astype(bf16)
            return carry

        lax.fori_loop(0, 2 * W, one, 0, unroll=True)

    outer = lambda t: t + (t // W) * R
    inner = lambda t: t + W
    sweep(outer, edge)
    for d in range(2):
        for e in range(2):
            when(s_has[d] & c_has[e], lambda: corner2(d, e).start())
    sweep(inner, edge)
    sweep(outer, range(W, C + W))
    for d in range(2):
        when(s_has[d], lambda: stream2(d).start())

    for e in range(2):
        @pl.when(c_has[e])
        def _():
            for d in range(2):
                when(s_has[1 - d], lambda: corner2(d, e).wait_recv())
            for i in range(R):
                for j in range(W):
                    col = e * (C + W) + j
                    msum[i, e * W + j] = (
                        fix4[i + W, col].astype(f32) + rs[i, col].astype(f32)).astype(bf16)
            cross2(e).start()

    for k in range(1, ns):
        share(k, lax.rem(s + ns - k, ns)).wait_recv()

    def own(i, carry):
        for j in range(C):
            values = coarse_all[aggregate[i, j]]
            spread = jnp.concatenate(
                [jnp.broadcast_to(values[f:f + 1], (width // 4, sides)) for f in range(4)], axis=0)
            out[i, j] = fix_of(i + W, j + W) + spread
        return carry

    lax.fori_loop(0, R, own, 0, unroll=True)

    for d in range(2):
        when(s_has[1 - d], lambda: stream2(d).wait_recv())
    for e in range(2):
        when(c_has[1 - e], lambda: cross2(e).wait_recv())

    def finish(i, carry):
        for j in range(C):
            value = out[i, j] + rs[i, j + W].astype(f32)
            if j < W:
                value = value + rc[i, j].astype(f32)
            if j >= C - W:
                value = value + rc[i, j - C + 2 * W].astype(f32)
            keep = jnp.full(value.shape, i * C + j, jnp.int32) < live
            out[i, j] = jnp.where(keep, value, 0.0)
        return carry

    lax.fori_loop(0, R, finish, 0, unroll=True)

    for e in range(2):
        @pl.when(c_has[e])
        def _():
            cross1(e).wait_send()
            cross2(e).wait_send()
    for d in range(2):
        @pl.when(s_has[d])
        def _():
            stream1(d).wait_send()
            stream2(d).wait_send()
            for e in range(2):
                @pl.when(c_has[e])
                def _():
                    corner1(d, e).wait_send()
                    corner2(d, e).wait_send()
    for k in range(1, ns):
        give(k).wait_send()
        share(k, s).wait_send()


def body(ns, nc, residual, approx_inverse, pattern, live_blocks, block_aggregate, coarse_inverse):
    R, C, width, sides = residual.shape
    _, extent, _, depth = approx_inverse.shape
    owned = coarse_inverse.shape[0] // 4
    bf16, f32 = jnp.bfloat16, jnp.float32
    dma = pltpu.SemaphoreType.DMA
    hbm = pl.BlockSpec(memory_space=pl.ANY)
    smem = pl.BlockSpec(memory_space=pltpu.SMEM)
    vmem = pl.BlockSpec(memory_space=pltpu.VMEM)
    RE, CE = R + 2 * W, C + 2 * W
    return pl.pallas_call(
        functools.partial(kernel, ns, nc, R, C),
        out_shape=jax.ShapeDtypeStruct(residual.shape, f32),
        in_specs=[hbm, hbm, smem, smem, smem, vmem],
        out_specs=vmem,
        scratch_shapes=[
            pltpu.VMEM(residual.shape, bf16),
            pltpu.VMEM((extent, width, depth), bf16),
            pltpu.VMEM((RE, CE, width, sides), bf16),
            pltpu.VMEM((RE, CE, width, sides), bf16),
            pltpu.VMEM((2 * W, CE, width, sides), bf16),
            pltpu.VMEM((R, 2 * W, width, sides), bf16),
            pltpu.VMEM((R, 2 * W, width, sides), bf16),
            pltpu.VMEM((R * C * 4, sides), f32),
            pltpu.VMEM((ns, 4 * owned, sides), f32),
            pltpu.VMEM((ns - 1, 4 * owned, sides), f32),
            pltpu.VMEM((ns * owned, 4, sides), f32),
            dma((2,)),
            dma((4,)), dma((4,)), dma((4,)), dma((4,)),
            dma((ns - 1,)), dma((ns - 1,)), dma((ns - 1,)), dma((ns - 1,)),
            dma((4,)), dma((4,)), dma((4,)), dma((4,)),
        ],
        compiler_params=pltpu.CompilerParams(
            collective_id=0, has_side_effects=True, vmem_limit_bytes=40 * 1024 * 1024),
        cost_estimate=pl.CostEstimate(
            flops=2 * extent * width * depth * sides,
            bytes_accessed=extent * width * depth * 2 + residual.size * 6,
            transcendentals=0),
    )(residual, approx_inverse, pattern, live_blocks, block_aggregate, coarse_inverse)


def solution(mesh):
    placed = (
        P("stream", "cross", None, None),
        P("stream", "cross", None, None),
        P("stream", "cross", None),
        P("stream", "cross"),
        P("stream", "cross"),
        P("stream", "cross"),
    )
    return jax.shard_map(
        functools.partial(body, mesh.shape["stream"], mesh.shape["cross"]),
        mesh=mesh,
        in_specs=placed,
        out_specs=P("stream", "cross", None, None),
        check_vma=False,
    )
```

time: 98.1 us -> 31.6 us (0.32); the launches traced: 96.3 us -> 31.3 us
  Pallas kernels: 0 us -> 24.5 us
  starting transfers between devices: 23.5 us -> 0 us
  waiting for transfers between devices: 22.1 us -> 0 us
  between operations: 14.5 us -> 0.67 us
  other arithmetic: 12.6 us -> 0 us
  matrix products: 7.99 us -> 0 us
  blocking collectives: 5.92 us -> 0 us
  local copies, waits for them, and re-layouts: 9.72 us -> 6.08 us
    pallas_call x0 -> x1, Pallas kernels: none -> 24.5 us  [body(): pl.pallas_call(functools.partial(kernel, ns, nc, R, C), out_shape=jax.Sha...]
    ppermute x8 -> x0, starting transfers between devices: 23.5 us -> none  [the longest x4 13.7 us: with_halo(): lax.ppermute(tail, axis, [(i, (i + 1) % count) for i in range(ends)])]
    ppermute x8 -> x0, waiting for transfers between devices: 15.5 us -> none  [the longest x4 8.59 us: with_halo(): lax.ppermute(tail, axis, [(i, (i + 1) % count) for i in range(ends)])]
    dot_general x4 -> x0, matrix products: 7.99 us -> none  [the longest x1 4.02 us: body(): jnp.einsum('nac,ncr->nar', blocks, picked, preferred_element_type=jnp.flo...]
    reduce_scatter x1 -> x0, waiting for transfers between devices: 6.66 us -> none  [body(): lax.psum_scatter(jnp.dot(chosen.T, per_block, precision=lax.Precision.HIG...]
    all_gather x1 -> x0, blocking collectives: 5.92 us -> none  [body(): lax.all_gather(coarse, 'stream', axis=0, tiled=True)]
    gather x1 -> x0, local copies, waits for them, and re-layouts: 5.43 us -> none  [body(): extended.reshape(extent, width, sides)[links].reshape(extent, depth, sides)]
    unnamed x24 -> x10, local copies, waits for them, and re-layouts: 1.56 us -> 6.08 us
  transfers between devices with their start and end apart: 9 -> 0, of which waited for: 7 -> 0; matrix products, arithmetic and copies ran while one was open for 8% -> 0% of each run, Pallas kernels for 0% -> 0%
where the time goes in v1:
time: 31.6 us; the launch traced here: 31.3 us
  Pallas kernels  24.5 us (78%)
  local copies, waits for them, and re-layouts  6.08 us (19%)
  between operations  0.67 us (2%)
    pallas_call x1, Pallas kernels, body(): pl.pallas_call(functools.partial(kernel, ns, nc, R, C), out_shape=jax.Sha...  24.5 us
    unnamed x10, local copies, waits for them, and re-layouts  6.08 us

profile of v1, /device:TPU:17, one launch (start us, length us, event | category | flops | bytes accessed | tf_op | source)
XLA Modules:
  0.0 31.3 jit_solution(14593373667631094499)
XLA Ops:
  0.7 0.8 %copy.7.pattern = s32[1,96,4]{2,1,0:T(8,128)S(1)} copy(s32[1,96,4]{1,2,0:T(4,128)} %param.8) | data formatting | bytes 3072 | tf_op args[2]
  1.4 0.0 copy-start
  1.4 1.9 %copy-done = bf16[1,96,64,256]{3,2,1,0:T(8,128)(2,1)S(1)} copy-done((bf16[1,96,64,256]{3,2,1,0:T(8,128)(2,1)S(1)}, bf16[1,96,64,256]{3,2,1,0:T(8,128)(2,1)}, u32[]{:S(2)}) %copy-start) | copy-done | bytes 3145752
  3.3 0.0 copy-start.1
  3.3 1.0 %copy-done.1 = bf16[4,8,64,128]{3,2,1,0:T(8,128)(2,1)S(1)} copy-done((bf16[4,8,64,128]{3,2,1,0:T(8,128)(2,1)S(1)}, bf16[4,8,64,128]{3,2,1,0:T(8,128)(2,1)}, u32[]{:S(2)}) %copy-start.1) | copy-done | bytes 524312
  4.4 0.0 copy-start.2
  4.4 0.7 %copy-done.2 = f32[32,32]{1,0:T(8,128)S(1)} copy-done((f32[32,32]{1,0:T(8,128)S(1)}, f32[32,32]{1,0:T(8,128)}, u32[]{:S(2)}) %copy-start.2) | copy-done | bytes 4120
  5.1 0.0 copy-start.3
  5.1 0.7 %copy-done.3 = s32[4,8]{1,0:T(4,128)S(1)} copy-done((s32[4,8]{1,0:T(4,128)S(1)}, s32[4,8]{1,0:T(4,128)}, u32[]{:S(2)}) %copy-start.3) | copy-done | bytes 152
  5.8 24.5 %shard_map.64 = f32[4,8,64,128]{3,2,1,0:T(8,128)S(1)} custom-call(bf16[4,8,64,128]{3,2,1,0:T(8,128)(2,1)S(1)} %copy-done.1, bf16[1,96,64,256]{3,2,1,0:T(8,128)(2,1)S(1)} %copy-done, s32[1,96,4]{2,1,0:T(8,128)S(1)} %copy.7.pattern, s32[1,1]{1,0:T(1,128)S(6)} %copy.9.live_ref, s32[4,8]{1,0:T(4,128)S(1)} %copy-done.3, f32[32,32]{1,0:T(8,128)S(1)} %copy-done.2), custom_call_target="tpu_custom_call" | custom-call | flops 402653184 | bytes 4718592 | tf_op jit(solution)/shard_map/pallas_call | solution.py:298
  30.3 1.0 %copy.10 = f32[4,8,64,128]{3,2,1,0:T(8,128)} copy(f32[4,8,64,128]{3,2,1,0:T(8,128)S(1)} %shard_map.64) | data formatting | bytes 2097152
Async XLA Ops:
  1.4 1.9 %copy-start = (bf16[1,96,64,256]{3,2,1,0:T(8,128)(2,1)S(1)}, bf16[1,96,64,256]{3,2,1,0:T(8,128)(2,1)}, u32[]{:S(2)}) copy-start(bf16[1,96,64,256]{3,2,1,0:T(8,128)(2,1)} %inverse.1) | copy-start | bytes 9437188
  3.3 1.0 %copy-start.1 = (bf16[4,8,64,128]{3,2,1,0:T(8,128)(2,1)S(1)}, bf16[4,8,64,128]{3,2,1,0:T(8,128)(2,1)}, u32[]{:S(2)}) copy-start(bf16[4,8,64,128]{3,2,1,0:T(8,128)(2,1)} %residual.1) | copy-start | bytes 1572868
  4.4 0.7 %copy-start.2 = (f32[32,32]{1,0:T(8,128)S(1)}, f32[32,32]{1,0:T(8,128)}, u32[]{:S(2)}) copy-start(f32[32,32]{1,0:T(8,128)} %coarse_inv.1) | copy-start | bytes 12292
  5.1 0.7 %copy-start.3 = (s32[4,8]{1,0:T(4,128)S(1)}, s32[4,8]{1,0:T(4,128)}, u32[]{:S(2)}) copy-start(s32[4,8]{1,0:T(4,128)} %aggregate.1) | copy-start | bytes 388

commit v2 on v1

v2 whole, which is shorter than its diff:
```python
import functools

import jax
import jax.numpy as jnp
from jax import lax
from jax.experimental import pallas as pl
from jax.experimental.pallas import tpu as pltpu
from jax.sharding import PartitionSpec as P

W = 2


def kernel(
    ns, nc, R, C,
    residual, inverse, pattern_in, live_in, aggregate_in, coarse_in,
    out,
    res, a_mat, pattern, live_ref, aggregate, coarse_inv,
    ext4, fix4, rs, rc, msum, pb, partial, part_in, coarse_all,
    in_sem, h_send, h_recv, t_send, t_recv, q_send, q_recv, p_send, p_recv, g_send, g_recv,
    b_send, b_recv, d_send, d_recv, m_send, m_recv,
):
    s = lax.axis_index("stream")
    c = lax.axis_index("cross")
    width, sides = res.shape[2], res.shape[3]
    CE = C + 2 * W
    RE = R + 2 * W
    owned = coarse_inv.shape[0] // 4
    bf16, f32 = jnp.bfloat16, jnp.float32

    far = lax.rem(s, 2)
    near = 1 - far

    def s_has(d):
        to = s + 2 * d - 1
        return (to >= 0) & (to < ns)

    def c_has(e):
        return c > 0 if e == 0 else c < nc - 1

    def s_to(d):
        return {"stream": jnp.clip(s + 2 * d - 1, 0, ns - 1)}

    def c_to(e):
        return {"cross": jnp.clip(c + 2 * e - 1, 0, nc - 1)}

    loads = [
        pltpu.make_async_copy(residual, res, in_sem.at[0]),
        pltpu.make_async_copy(live_in, live_ref, in_sem.at[1]),
        pltpu.make_async_copy(aggregate_in, aggregate, in_sem.at[2]),
        pltpu.make_async_copy(coarse_in, coarse_inv, in_sem.at[3]),
        pltpu.make_async_copy(pattern_in, pattern, in_sem.at[4]),
        pltpu.make_async_copy(inverse.at[0], a_mat, in_sem.at[5]),
    ]
    for load in loads:
        load.start()

    barrier = pltpu.get_barrier_semaphore()
    for e in range(2):
        @pl.when(c_has(e))
        def _():
            pl.semaphore_signal(barrier, inc=1, device_id=c_to(e),
                                device_id_type=pl.DeviceIdType.MESH)
    for k in range(1, ns):
        pl.semaphore_signal(barrier, inc=1, device_id={"stream": lax.rem(s + k, ns)},
                            device_id_type=pl.DeviceIdType.MESH)

    def zero(ref, rows, cols):
        ref[rows[0]:rows[1], cols[0]:cols[1]] = jnp.zeros(
            (rows[1] - rows[0], cols[1] - cols[0], width, sides), bf16)

    @pl.when(s == 0)
    def _():
        zero(ext4, (0, W), (0, CE))
        zero(rs, (0, W), (0, CE))

    @pl.when(s == ns - 1)
    def _():
        zero(ext4, (R + W, RE), (0, CE))
        zero(rs, (W, 2 * W), (0, CE))

    @pl.when(c == 0)
    def _():
        zero(ext4, (0, RE), (0, W))
        zero(rc, (0, R), (0, W))

    @pl.when(c == nc - 1)
    def _():
        zero(ext4, (0, RE), (C + W, CE))
        zero(rc, (0, R), (W, 2 * W))

    loads[1].wait()
    live = live_ref[0, 0]
    loads[0].wait()

    def mask_row(i, carry):
        for j in range(C):
            block = res[i, j]
            keep = jnp.full(block.shape, i * C + j, jnp.int32) < live
            ext4[i + W, j + W] = jnp.where(keep, block.astype(f32), 0.0).astype(bf16)
        return carry

    lax.fori_loop(0, R, mask_row, 0, unroll=True)

    own_cols = (pl.ds(W, W), pl.ds(C, W))
    halo_cols = (pl.ds(C + W, W), pl.ds(0, W))
    side_cols = (pl.ds(0, W), pl.ds(C + W, W))
    mid_cols = pl.ds(W, C)

    def remote(src, dst, send, recv, to):
        return pltpu.make_async_remote_copy(
            src_ref=src, dst_ref=dst, send_sem=send, recv_sem=recv,
            device_id=to, device_id_type=pl.DeviceIdType.MESH)

    def own_rows(d):
        return pl.ds(W + W * d, W)

    def halo_rows(d):
        return pl.ds((1 - d) * (R + W), W)

    def cross1(e, d):
        i = 2 * e + d
        return remote(ext4.at[own_rows(d), own_cols[e]], ext4.at[own_rows(d), halo_cols[e]],
                      h_send.at[i], h_recv.at[i], c_to(e))

    def stream1(d):
        return remote(ext4.at[own_rows(d), mid_cols], ext4.at[halo_rows(d), mid_cols],
                      t_send.at[d], t_recv.at[d], s_to(d))

    def corner1(d, e):
        i = 2 * e + d
        return remote(ext4.at[own_rows(d), side_cols[e]], ext4.at[halo_rows(d), side_cols[e]],
                      q_send.at[i], q_recv.at[i], s_to(d))

    def far_rows(d):
        return pl.ds(d * (R + W), W)

    def corner2(d, e):
        i = 2 * e + d
        return remote(fix4.at[far_rows(d), side_cols[e]], rs.at[pl.ds(W * (1 - d), W), side_cols[e]],
                      b_send.at[i], b_recv.at[i], s_to(d))

    def stream2(d):
        return remote(fix4.at[far_rows(d), mid_cols], rs.at[pl.ds(W * (1 - d), W), mid_cols],
                      d_send.at[d], d_recv.at[d], s_to(d))

    def cross2(e, d):
        i = 2 * e + d
        return remote(msum.at[pl.ds(W * d, W), pl.ds(W * e, W)],
                      rc.at[pl.ds(W * d, W), pl.ds(W * (1 - e), W)],
                      m_send.at[i], m_recv.at[i], c_to(e))

    def when(cond, run):
        pl.when(cond)(run)

    pl.semaphore_wait(barrier, ns - 1 + c_has(0).astype(jnp.int32) + c_has(1).astype(jnp.int32))

    for d in (far, near):
        for e in range(2):
            when(c_has(e), lambda: cross1(e, d).start())
        when(s_has(d), lambda: stream1(d).start())

    def sums(m, carry):
        i = m // (C // 2)
        j = (m % (C // 2)) * 2
        rows = []
        for t in range(2):
            block = ext4[i + W, j + W + t].astype(f32)
            rows.append(block.reshape(4, width // 4, sides).sum(axis=1))
        pb[pl.ds(pl.multiple_of(m * 8, 8), 8), :] = jnp.concatenate(rows, axis=0)
        return carry

    lax.fori_loop(0, R * C // 2, sums, 0, unroll=True)
    loads[2].wait()
    n_own = R * C
    lane = lax.broadcasted_iota(jnp.int32, (8, 4 * n_own), 1)
    key = jnp.zeros((8, 4 * n_own), jnp.int32)
    for i in range(R):
        for j in range(C):
            key = jnp.where(lane // 4 == i * C + j, aggregate[i, j], key)
    key = (key * 4 + lane % 4)[0:1]
    for o in range(ns):
        row = lax.broadcasted_iota(jnp.int32, (4 * owned, 4 * n_own), 0) + o * 4 * owned
        chosen = (row == jnp.broadcast_to(key, row.shape)).astype(f32)
        partial[o] = jnp.dot(chosen, pb[...], precision=lax.Precision.HIGHEST,
                             preferred_element_type=f32)

    def give(k):
        to = lax.rem(s + k, ns)
        return remote(partial.at[to], part_in.at[k - 1], p_send.at[k - 1], p_recv.at[k - 1],
                      {"stream": to})

    def share(k, mine):
        part = coarse_all.at[pl.ds(mine * owned, owned)]
        return remote(part, part, g_send.at[k - 1], g_recv.at[k - 1],
                      {"stream": lax.rem(s + k, ns)})

    for k in range(1, ns):
        give(k).start()

    for e in range(2):
        when(c_has(1 - e), lambda: cross1(e, far).wait_recv())
    for e in range(2):
        when(s_has(far) & c_has(e), lambda: corner1(far, e).start())

    loads[3].wait()
    total = partial[s]
    for k in range(1, ns):
        give(k).wait_recv()
        total = total + part_in[k - 1]
    coarse = jnp.dot(coarse_inv[...], total, precision=lax.Precision.HIGHEST,
                     preferred_element_type=f32)
    for a in range(owned):
        coarse_all[s * owned + a] = coarse[4 * a:4 * a + 4]
    for k in range(1, ns):
        share(k, s).start()

    for e in range(2):
        when(c_has(1 - e), lambda: cross1(e, near).wait_recv())
    for e in range(2):
        when(s_has(near) & c_has(e), lambda: corner1(near, e).start())

    loads[4].wait()
    loads[5].wait()
    for d in range(2):
        when(s_has(1 - d), lambda: stream1(d).wait_recv())
    for d in (near, far):
        for e in range(2):
            when(s_has(1 - d) & c_has(e), lambda: corner1(d, e).wait_recv())

    ext = ext4.reshape(RE * CE, width, sides)

    def fix_of(i, j):
        n = i * CE + j
        picked = jnp.concatenate(
            [ext[pattern[0, k, n]] for k in range(a_mat.shape[2] // width)], axis=0)
        return jnp.dot(a_mat[n], picked, preferred_element_type=f32)

    edge = tuple(range(W)) + tuple(range(C + W, CE))
    middle = tuple(range(W, C + W))

    def sweep(first, cols):
        def one(t, carry):
            for j in cols:
                fix4[first + t, j] = fix_of(first + t, j).astype(bf16)
            return carry

        lax.fori_loop(0, W, one, 0, unroll=True)

    def fold(d):
        for e in range(2):
            @pl.when(c_has(e))
            def _():
                when(s_has(d), lambda: corner2(1 - d, e).wait_recv())
                for t in range(W):
                    i = W * d + t
                    for j in range(W):
                        col = e * (C + W) + j
                        msum[i, e * W + j] = (
                            fix4[i + W, col].astype(f32) + rs[i, col].astype(f32)).astype(bf16)
                cross2(e, d).start()

    for d in (far, near):
        sweep(d * (R + W), edge)
        for e in range(2):
            when(s_has(d) & c_has(e), lambda: corner2(d, e).start())
    sweep(W + W * near, edge)
    fold(near)
    sweep(W + W * far, edge)
    for d in (far, near):
        sweep(d * (R + W), middle)
        when(s_has(d), lambda: stream2(d).start())
    fold(far)

    for k in range(1, ns):
        share(k, lax.rem(s + ns - k, ns)).wait_recv()

    def own(i, carry):
        for j in range(C):
            values = coarse_all[aggregate[i, j]]
            spread = jnp.concatenate(
                [jnp.broadcast_to(values[f:f + 1], (width // 4, sides)) for f in range(4)], axis=0)
            out[i, j] = fix_of(i + W, j + W) + spread
        return carry

    lax.fori_loop(0, R, own, 0, unroll=True)

    for d in range(2):
        when(s_has(1 - d), lambda: stream2(d).wait_recv())

    def kept(i, j, value):
        keep = jnp.full(value.shape, i * C + j, jnp.int32) < live
        return jnp.where(keep, value, 0.0)

    def add_stream(i, carry):
        for j in range(C):
            out[i, j] = kept(i, j, out[i, j] + rs[i, j + W].astype(f32))
        return carry

    lax.fori_loop(0, R, add_stream, 0, unroll=True)

    def add_cross(d):
        for e in range(2):
            when(c_has(1 - e), lambda: cross2(e, d).wait_recv())
        for t in range(W):
            i = W * d + t
            for j in range(W):
                for col, at in ((j, j), (C - W + j, W + j)):
                    out[i, col] = kept(i, col, out[i, col] + rc[i, at].astype(f32))

    add_cross(near)
    add_cross(far)

    for e in range(2):
        @pl.when(c_has(e))
        def _():
            for d in range(2):
                cross1(e, d).wait_send()
                cross2(e, d).wait_send()
    for d in range(2):
        @pl.when(s_has(d))
        def _():
            stream1(d).wait_send()
            stream2(d).wait_send()
            for e in range(2):
                @pl.when(c_has(e))
                def _():
                    corner1(d, e).wait_send()
                    corner2(d, e).wait_send()
    for k in range(1, ns):
        give(k).wait_send()
        share(k, s).wait_send()


def body(ns, nc, residual, approx_inverse, pattern, live_blocks, block_aggregate, coarse_inverse):
    R, C, width, sides = residual.shape
    _, extent, _, depth = approx_inverse.shape
    owned = coarse_inverse.shape[0] // 4
    bf16, f32, i32 = jnp.bfloat16, jnp.float32, jnp.int32
    dma = pltpu.SemaphoreType.DMA
    hbm = pl.BlockSpec(memory_space=pltpu.HBM)
    vmem = pl.BlockSpec(memory_space=pltpu.VMEM)
    RE, CE = R + 2 * W, C + 2 * W
    links = jnp.transpose(pattern, (0, 2, 1))
    return pl.pallas_call(
        functools.partial(kernel, ns, nc, R, C),
        out_shape=jax.ShapeDtypeStruct(residual.shape, f32),
        in_specs=[hbm] * 6,
        out_specs=vmem,
        scratch_shapes=[
            pltpu.VMEM(residual.shape, bf16),
            pltpu.VMEM((extent, width, depth), bf16),
            pltpu.SMEM(links.shape, i32),
            pltpu.SMEM(live_blocks.shape, i32),
            pltpu.SMEM(block_aggregate.shape, i32),
            pltpu.VMEM(coarse_inverse.shape, f32),
            pltpu.VMEM((RE, CE, width, sides), bf16),
            pltpu.VMEM((RE, CE, width, sides), bf16),
            pltpu.VMEM((2 * W, CE, width, sides), bf16),
            pltpu.VMEM((R, 2 * W, width, sides), bf16),
            pltpu.VMEM((R, 2 * W, width, sides), bf16),
            pltpu.VMEM((R * C * 4, sides), f32),
            pltpu.VMEM((ns, 4 * owned, sides), f32),
            pltpu.VMEM((ns - 1, 4 * owned, sides), f32),
            pltpu.VMEM((ns * owned, 4, sides), f32),
            dma((6,)),
            dma((4,)), dma((4,)), dma((2,)), dma((2,)), dma((4,)), dma((4,)),
            dma((ns - 1,)), dma((ns - 1,)), dma((ns - 1,)), dma((ns - 1,)),
            dma((4,)), dma((4,)), dma((2,)), dma((2,)), dma((4,)), dma((4,)),
        ],
        compiler_params=pltpu.CompilerParams(
            collective_id=0, has_side_effects=True, vmem_limit_bytes=60 * 1024 * 1024),
        cost_estimate=pl.CostEstimate(
            flops=2 * extent * width * depth * sides,
            bytes_accessed=extent * width * depth * 2 + residual.size * 6,
            transcendentals=0),
    )(residual, approx_inverse, links, live_blocks, block_aggregate, coarse_inverse)


def solution(mesh):
    placed = (
        P("stream", "cross", None, None),
        P("stream", "cross", None, None),
        P("stream", "cross", None),
        P("stream", "cross"),
        P("stream", "cross"),
        P("stream", "cross"),
    )
    return jax.shard_map(
        functools.partial(body, mesh.shape["stream"], mesh.shape["cross"]),
        mesh=mesh,
        in_specs=placed,
        out_specs=P("stream", "cross", None, None),
        check_vma=False,
    )
```

time: 31.6 us -> 25 us (0.79)
  local copies, waits for them, and re-layouts: 6.08 us -> 2.31 us
  Pallas kernels: 24.5 us -> 21.8 us
    unnamed x10 -> x1, local copies, waits for them, and re-layouts: 6.08 us -> 2.31 us
    pallas_call x1, Pallas kernels: 24.5 us -> 21.8 us  [body(): pl.pallas_call(functools.partial(kernel, ns, nc, R, C), out_shape=jax.Sha...]
where the time goes in v2:
time: 25 us; the launch traced here: 24.8 us
  Pallas kernels  21.8 us (87%)
  local copies, waits for them, and re-layouts  2.31 us (9%)
  between operations  0.66 us (3%)
    pallas_call x1, Pallas kernels, body(): pl.pallas_call(functools.partial(kernel, ns, nc, R, C), out_shape=jax.Sha...  21.8 us
    unnamed x1, local copies, waits for them, and re-layouts  2.31 us

profile of v2, /device:TPU:17, one launch (start us, length us, event | category | flops | bytes accessed | tf_op | source)
XLA Modules:
  0.0 24.8 jit_solution(9666685172392766210)
XLA Ops:
  0.7 21.8 %shard_map.64 = f32[4,8,64,128]{3,2,1,0:T(8,128)} custom-call(bf16[4,8,64,128]{3,2,1,0:T(8,128)(2,1)} %residual.1, bf16[1,96,64,256]{3,2,1,0:T(8,128)(2,1)} %inverse.1, s32[1,4,96]{2,1,0:T(4,128)} %bitcast.1, s32[1,1]{1,0:T(1,128)S(6)} %copy.8.live_in, s32[4,8]{1,0:T(4,128)} %aggregate_in.1, f32[32,32]{1,0:T(8,128)} %coarse_in.1), custom_call_target="tpu_custom_call" | custom-call | flops 402653184 | bytes 4718592 | tf_op jit(solution)/shard_map/pallas_call | solution.py:344
  22.5 2.3 %copy.9 = f32[4,8,64,128]{3,2,1,0:T(8,128)} copy(f32[4,8,64,128]{3,2,1,0:T(8,128)} %shard_map.64) | data formatting | bytes 2097152

commit v3 on v2

--- a/solution.py
+++ b/solution.py
@@ -12,9 +12,9 @@
 
 def kernel(
     ns, nc, R, C,
-    residual, inverse, pattern_in, live_in, aggregate_in, coarse_in,
+    live_ref, residual, inverse, pattern_in, aggregate_in, coarse_in,
     out,
-    res, a_mat, pattern, live_ref, aggregate, coarse_inv,
+    res, a_mat, pattern, aggregate, coarse_inv,
     ext4, fix4, rs, rc, msum, pb, partial, part_in, coarse_all,
     in_sem, h_send, h_recv, t_send, t_recv, q_send, q_recv, p_send, p_recv, g_send, g_recv,
     b_send, b_recv, d_send, d_recv, m_send, m_recv,
@@ -45,11 +45,10 @@
 
     loads = [
         pltpu.make_async_copy(residual, res, in_sem.at[0]),
-        pltpu.make_async_copy(live_in, live_ref, in_sem.at[1]),
-        pltpu.make_async_copy(aggregate_in, aggregate, in_sem.at[2]),
-        pltpu.make_async_copy(coarse_in, coarse_inv, in_sem.at[3]),
-        pltpu.make_async_copy(pattern_in, pattern, in_sem.at[4]),
-        pltpu.make_async_copy(inverse.at[0], a_mat, in_sem.at[5]),
+        pltpu.make_async_copy(aggregate_in, aggregate, in_sem.at[1]),
+        pltpu.make_async_copy(coarse_in, coarse_inv, in_sem.at[2]),
+        pltpu.make_async_copy(pattern_in, pattern, in_sem.at[3]),
+        pltpu.make_async_copy(inverse.at[0], a_mat, in_sem.at[4]),
     ]
     for load in loads:
         load.start()
@@ -88,18 +87,20 @@
         zero(ext4, (0, RE), (C + W, CE))
         zero(rc, (0, R), (W, 2 * W))
 
-    loads[1].wait()
     live = live_ref[0, 0]
     loads[0].wait()
 
-    def mask_row(i, carry):
-        for j in range(C):
-            block = res[i, j]
-            keep = jnp.full(block.shape, i * C + j, jnp.int32) < live
-            ext4[i + W, j + W] = jnp.where(keep, block.astype(f32), 0.0).astype(bf16)
-        return carry
-
-    lax.fori_loop(0, R, mask_row, 0, unroll=True)
+    def mask(cols):
+        def row(i, carry):
+            for j in cols:
+                block = res[i, j]
+                keep = jnp.full(block.shape, i * C + j, jnp.int32) < live
+                ext4[i + W, j + W] = jnp.where(keep, block.astype(f32), 0.0).astype(bf16)
+            return carry
+
+        lax.fori_loop(0, R, row, 0, unroll=True)
+
+    mask(tuple(range(W)) + tuple(range(C - W, C)))
 
     own_cols = (pl.ds(W, W), pl.ds(C, W))
     halo_cols = (pl.ds(C + W, W), pl.ds(0, W))
@@ -157,6 +158,8 @@
     for d in (far, near):
         for e in range(2):
             when(c_has(e), lambda: cross1(e, d).start())
+    mask(range(W, C - W))
+    for d in (far, near):
         when(s_has(d), lambda: stream1(d).start())
 
     def sums(m, carry):
@@ -170,7 +173,7 @@
         return carry
 
     lax.fori_loop(0, R * C // 2, sums, 0, unroll=True)
-    loads[2].wait()
+    loads[1].wait()
     n_own = R * C
     lane = lax.broadcasted_iota(jnp.int32, (8, 4 * n_own), 1)
     key = jnp.zeros((8, 4 * n_own), jnp.int32)
@@ -202,7 +205,7 @@
     for e in range(2):
         when(s_has(far) & c_has(e), lambda: corner1(far, e).start())
 
-    loads[3].wait()
+    loads[2].wait()
     total = partial[s]
     for k in range(1, ns):
         give(k).wait_recv()
@@ -219,8 +222,8 @@
     for e in range(2):
         when(s_has(near) & c_has(e), lambda: corner1(near, e).start())
 
+    loads[3].wait()
     loads[4].wait()
-    loads[5].wait()
     for d in range(2):
         when(s_has(1 - d), lambda: stream1(d).wait_recv())
     for d in (near, far):
@@ -259,17 +262,18 @@
                             fix4[i + W, col].astype(f32) + rs[i, col].astype(f32)).astype(bf16)
                 cross2(e, d).start()
 
-    for d in (far, near):
+    for d in (near, far):
         sweep(d * (R + W), edge)
         for e in range(2):
             when(s_has(d) & c_has(e), lambda: corner2(d, e).start())
     sweep(W + W * near, edge)
     fold(near)
     sweep(W + W * far, edge)
-    for d in (far, near):
-        sweep(d * (R + W), middle)
-        when(s_has(d), lambda: stream2(d).start())
+    sweep(far * (R + W), middle)
+    when(s_has(far), lambda: stream2(far).start())
     fold(far)
+    sweep(near * (R + W), middle)
+    when(s_has(near), lambda: stream2(near).start())
 
     for k in range(1, ns):
         share(k, lax.rem(s + ns - k, ns)).wait_recv()
@@ -341,16 +345,16 @@
     vmem = pl.BlockSpec(memory_space=pltpu.VMEM)
     RE, CE = R + 2 * W, C + 2 * W
     links = jnp.transpose(pattern, (0, 2, 1))
+    operands = (residual, approx_inverse, links, block_aggregate, coarse_inverse)
     return pl.pallas_call(
         functools.partial(kernel, ns, nc, R, C),
-        out_shape=jax.ShapeDtypeStruct(residual.shape, f32),
-        in_specs=[hbm] * 6,
+        out_shape=pltpu.VMEM(residual.shape, f32),
+        in_specs=[pl.BlockSpec(memory_space=pltpu.SMEM)] + [hbm] * 5,
         out_specs=vmem,
         scratch_shapes=[
             pltpu.VMEM(residual.shape, bf16),
             pltpu.VMEM((extent, width, depth), bf16),
             pltpu.SMEM(links.shape, i32),
-            pltpu.SMEM(live_blocks.shape, i32),
             pltpu.SMEM(block_aggregate.shape, i32),
             pltpu.VMEM(coarse_inverse.shape, f32),
             pltpu.VMEM((RE, CE, width, sides), bf16),
@@ -362,18 +366,18 @@
             pltpu.VMEM((ns, 4 * owned, sides), f32),
             pltpu.VMEM((ns - 1, 4 * owned, sides), f32),
             pltpu.VMEM((ns * owned, 4, sides), f32),
-            dma((6,)),
+            dma((5,)),
             dma((4,)), dma((4,)), dma((2,)), dma((2,)), dma((4,)), dma((4,)),
             dma((ns - 1,)), dma((ns - 1,)), dma((ns - 1,)), dma((ns - 1,)),
             dma((4,)), dma((4,)), dma((2,)), dma((2,)), dma((4,)), dma((4,)),
         ],
         compiler_params=pltpu.CompilerParams(
-            collective_id=0, has_side_effects=True, vmem_limit_bytes=60 * 1024 * 1024),
+            collective_id=0, has_side_effects=True, vmem_limit_bytes=40 * 1024 * 1024),
         cost_estimate=pl.CostEstimate(
             flops=2 * extent * width * depth * sides,
             bytes_accessed=extent * width * depth * 2 + residual.size * 6,
             transcendentals=0),
-    )(residual, approx_inverse, links, live_blocks, block_aggregate, coarse_inverse)
+    )(live_blocks, *(pltpu.with_memory_space_constraint(array, pltpu.HBM) for array in operands))
 
 
 def solution(mesh):

time: 25 us -> 22.6 us (0.904)
  local copies, waits for them, and re-layouts: 2.31 us -> 0.97 us
  Pallas kernels: 21.8 us -> 20.8 us
    unnamed x1, local copies, waits for them, and re-layouts: 2.31 us -> 0.97 us
    pallas_call x1, Pallas kernels: 21.8 us -> 20.8 us  [body(): pl.pallas_call(functools.partial(kernel, ns, nc, R, C), out_shape=pltpu.V...]
where the time goes in v3:
time: 22.6 us; the launch traced here: 22.4 us
  Pallas kernels  20.8 us (92%)
  local copies, waits for them, and re-layouts  0.97 us (4%)
  between operations  0.66 us (3%)
    pallas_call x1, Pallas kernels, body(): pl.pallas_call(functools.partial(kernel, ns, nc, R, C), out_shape=pltpu.V...  20.8 us
    unnamed x1, local copies, waits for them, and re-layouts  0.97 us

profile of v3, /device:TPU:17, one launch (start us, length us, event | category | flops | bytes accessed | tf_op | source)
XLA Modules:
  0.0 22.4 jit_solution(11042096771155569156)
XLA Ops:
  0.7 20.8 %shard_map.64 = f32[4,8,64,128]{3,2,1,0:T(8,128)S(1)} custom-call(s32[1,1]{1,0:T(1,128)S(6)} %copy.9.live_ref, bf16[4,8,64,128]{3,2,1,0:T(8,128)(2,1)} %residual.1, bf16[1,96,64,256]{3,2,1,0:T(8,128)(2,1)} %inverse.1, s32[1,4,96]{2,1,0:T(4,128)} %bitcast.1, s32[4,8]{1,0:T(4,128)} %aggregate_in.1, f32[32,32]{1,0:T(8,128)} %coarse_in.1), custom_call_target="tpu_custom_call" | custom-call | flops 402653184 | bytes 4718592 | tf_op jit(solution)/shard_map/pallas_call | solution.py:349
  21.5 1.0 %copy.8 = f32[4,8,64,128]{3,2,1,0:T(8,128)} copy(f32[4,8,64,128]{3,2,1,0:T(8,128)S(1)} %shard_map.64) | data formatting | bytes 2097152

commit v4 on v3

--- a/solution.py
+++ b/solution.py
@@ -181,11 +181,12 @@
         for j in range(C):
             key = jnp.where(lane // 4 == i * C + j, aggregate[i, j], key)
     key = (key * 4 + lane % 4)[0:1]
+    row = lax.broadcasted_iota(jnp.int32, (4 * owned * ns, 4 * n_own), 0)
+    chosen = (row == jnp.broadcast_to(key, row.shape)).astype(f32)
+    restricted = jnp.dot(chosen, pb[...], precision=lax.Precision.HIGHEST,
+                         preferred_element_type=f32)
     for o in range(ns):
-        row = lax.broadcasted_iota(jnp.int32, (4 * owned, 4 * n_own), 0) + o * 4 * owned
-        chosen = (row == jnp.broadcast_to(key, row.shape)).astype(f32)
-        partial[o] = jnp.dot(chosen, pb[...], precision=lax.Precision.HIGHEST,
-                             preferred_element_type=f32)
+        partial[o] = restricted[o * 4 * owned:(o + 1) * 4 * owned]
 
     def give(k):
         to = lax.rem(s + k, ns)
@@ -200,27 +201,12 @@
     for k in range(1, ns):
         give(k).start()
 
-    for e in range(2):
-        when(c_has(1 - e), lambda: cross1(e, far).wait_recv())
-    for e in range(2):
-        when(s_has(far) & c_has(e), lambda: corner1(far, e).start())
-
-    loads[2].wait()
-    total = partial[s]
-    for k in range(1, ns):
-        give(k).wait_recv()
-        total = total + part_in[k - 1]
-    coarse = jnp.dot(coarse_inv[...], total, precision=lax.Precision.HIGHEST,
-                     preferred_element_type=f32)
-    for a in range(owned):
-        coarse_all[s * owned + a] = coarse[4 * a:4 * a + 4]
-    for k in range(1, ns):
-        share(k, s).start()
-
-    for e in range(2):
-        when(c_has(1 - e), lambda: cross1(e, near).wait_recv())
-    for e in range(2):
-        when(s_has(near) & c_has(e), lambda: corner1(near, e).start())
+    for d in (far, near):
+        for e in range(2):
+            @pl.when(c_has(1 - e))
+            def _():
+                cross1(e, d).wait_recv()
+                when(s_has(d), lambda: corner1(d, 1 - e).start())
 
     loads[3].wait()
     loads[4].wait()
@@ -262,12 +248,26 @@
                             fix4[i + W, col].astype(f32) + rs[i, col].astype(f32)).astype(bf16)
                 cross2(e, d).start()
 
+    def coarse_step():
+        loads[2].wait()
+        total = partial[s]
+        for k in range(1, ns):
+            give(k).wait_recv()
+            total = total + part_in[k - 1]
+        coarse = jnp.dot(coarse_inv[...], total, precision=lax.Precision.HIGHEST,
+                         preferred_element_type=f32)
+        for a in range(owned):
+            coarse_all[s * owned + a] = coarse[4 * a:4 * a + 4]
+        for k in range(1, ns):
+            share(k, s).start()
+
     for d in (near, far):
         sweep(d * (R + W), edge)
         for e in range(2):
             when(s_has(d) & c_has(e), lambda: corner2(d, e).start())
     sweep(W + W * near, edge)
     fold(near)
+    coarse_step()
     sweep(W + W * far, edge)
     sweep(far * (R + W), middle)
     when(s_has(far), lambda: stream2(far).start())

time: 22.6 us -> 22.6 us (level)
  the two profiles are of different devices: /device:TPU:17 before, /device:TPU:21 now
where the time goes in v4:
time: 22.6 us; the launch traced here: 22.5 us
  Pallas kernels  20.8 us (92%)
  local copies, waits for them, and re-layouts  0.97 us (4%)
  between operations  0.66 us (3%)
    pallas_call x1, Pallas kernels, body(): pl.pallas_call(functools.partial(kernel, ns, nc, R, C), out_shape=pltpu.V...  20.8 us
    unnamed x1, local copies, waits for them, and re-layouts  0.97 us

profile of v4, /device:TPU:21, one launch (start us, length us, event | category | flops | bytes accessed | tf_op | source)
XLA Modules:
  0.0 22.5 jit_solution(2617403162611790778)
XLA Ops:
  0.7 20.8 %shard_map.64 = f32[4,8,64,128]{3,2,1,0:T(8,128)S(1)} custom-call(s32[1,1]{1,0:T(1,128)S(6)} %copy.9.live_ref, bf16[4,8,64,128]{3,2,1,0:T(8,128)(2,1)} %residual.1, bf16[1,96,64,256]{3,2,1,0:T(8,128)(2,1)} %inverse.1, s32[1,4,96]{2,1,0:T(4,128)} %bitcast.1, s32[4,8]{1,0:T(4,128)} %aggregate_in.1, f32[32,32]{1,0:T(8,128)} %coarse_in.1), custom_call_target="tpu_custom_call" | custom-call | flops 402653184 | bytes 4718592 | tf_op jit(solution)/shard_map/pallas_call | solution.py:349
  21.5 1.0 %copy.8 = f32[4,8,64,128]{3,2,1,0:T(8,128)} copy(f32[4,8,64,128]{3,2,1,0:T(8,128)S(1)} %shard_map.64) | data formatting | bytes 2097152

commit v5 on v4

--- a/solution.py
+++ b/solution.py
@@ -98,7 +98,7 @@
                 ext4[i + W, j + W] = jnp.where(keep, block.astype(f32), 0.0).astype(bf16)
             return carry
 
-        lax.fori_loop(0, R, row, 0, unroll=True)
+        lax.fori_loop(0, R, row, 0)
 
     mask(tuple(range(W)) + tuple(range(C - W, C)))
 
@@ -162,17 +162,17 @@
     for d in (far, near):
         when(s_has(d), lambda: stream1(d).start())
 
-    def sums(m, carry):
-        i = m // (C // 2)
-        j = (m % (C // 2)) * 2
-        rows = []
-        for t in range(2):
-            block = ext4[i + W, j + W + t].astype(f32)
-            rows.append(block.reshape(4, width // 4, sides).sum(axis=1))
-        pb[pl.ds(pl.multiple_of(m * 8, 8), 8), :] = jnp.concatenate(rows, axis=0)
+    def sums(i, carry):
+        for j in range(0, C, 2):
+            rows = []
+            for u in range(2):
+                block = ext4[i + W, j + W + u].astype(f32)
+                rows.append(block.reshape(4, width // 4, sides).sum(axis=1))
+            first = pl.multiple_of((i * C + j) * 4, 8)
+            pb[pl.ds(first, 8), :] = jnp.concatenate(rows, axis=0)
         return carry
 
-    lax.fori_loop(0, R * C // 2, sums, 0, unroll=True)
+    lax.fori_loop(0, R, sums, 0)
     loads[1].wait()
     n_own = R * C
     lane = lax.broadcasted_iota(jnp.int32, (8, 4 * n_own), 1)
@@ -227,13 +227,9 @@
     edge = tuple(range(W)) + tuple(range(C + W, CE))
     middle = tuple(range(W, C + W))
 
-    def sweep(first, cols):
-        def one(t, carry):
-            for j in cols:
-                fix4[first + t, j] = fix_of(first + t, j).astype(bf16)
-            return carry
-
-        lax.fori_loop(0, W, one, 0, unroll=True)
+    def put(i, cols):
+        for j in cols:
+            fix4[i, j] = fix_of(i, j).astype(bf16)
 
     def fold(d):
         for e in range(2):
@@ -261,46 +257,60 @@
         for k in range(1, ns):
             share(k, s).start()
 
-    for d in (near, far):
-        sweep(d * (R + W), edge)
-        for e in range(2):
-            when(s_has(d) & c_has(e), lambda: corner2(d, e).start())
-    sweep(W + W * near, edge)
-    fold(near)
-    coarse_step()
-    sweep(W + W * far, edge)
-    sweep(far * (R + W), middle)
-    when(s_has(far), lambda: stream2(far).start())
-    fold(far)
-    sweep(near * (R + W), middle)
-    when(s_has(near), lambda: stream2(near).start())
+    def edges(p, carry):
+        d = lax.rem(p, 2) * far + (1 - lax.rem(p, 2)) * near
+        first = jnp.where(p < 2, d * (R + W), W + W * d)
+        for u in range(W):
+            put(first + u, edge)
+
+        @pl.when(p < 2)
+        def _():
+            for e in range(2):
+                when(s_has(d) & c_has(e), lambda: corner2(d, e).start())
+
+        @pl.when(p == 2)
+        def _():
+            fold(near)
+            coarse_step()
+
+        return carry
+
+    lax.fori_loop(0, 4, edges, 0)
+
+    def rows(p, carry):
+        q = p // W
+        d = jnp.where(q == 0, far, near)
+        put(jnp.where(q < 2, d * (R + W) + lax.rem(p, W), p - W), middle)
+
+        @pl.when((lax.rem(p, W) == W - 1) & (q < 2))
+        def _():
+            when(s_has(d), lambda: stream2(d).start())
+            when(q == 0, lambda: fold(far))
+
+        return carry
+
+    lax.fori_loop(0, 2 * W + R, rows, 0)
 
     for k in range(1, ns):
         share(k, lax.rem(s + ns - k, ns)).wait_recv()
 
-    def own(i, carry):
+    for d in range(2):
+        when(s_has(1 - d), lambda: stream2(d).wait_recv())
+
+    def kept(i, j, value):
+        keep = jnp.full(value.shape, i * C + j, jnp.int32) < live
+        return jnp.where(keep, value, 0.0)
+
+    def add_stream(i, carry):
         for j in range(C):
             values = coarse_all[aggregate[i, j]]
             spread = jnp.concatenate(
                 [jnp.broadcast_to(values[f:f + 1], (width // 4, sides)) for f in range(4)], axis=0)
-            out[i, j] = fix_of(i + W, j + W) + spread
+            fine = fix4[i + W, j + W].astype(f32) + rs[i, j + W].astype(f32)
+            out[i, j] = kept(i, j, fine + spread)
         return carry
 
-    lax.fori_loop(0, R, own, 0, unroll=True)
-
-    for d in range(2):
-        when(s_has(1 - d), lambda: stream2(d).wait_recv())
-
-    def kept(i, j, value):
-        keep = jnp.full(value.shape, i * C + j, jnp.int32) < live
-        return jnp.where(keep, value, 0.0)
-
-    def add_stream(i, carry):
-        for j in range(C):
-            out[i, j] = kept(i, j, out[i, j] + rs[i, j + W].astype(f32))
-        return carry
-
-    lax.fori_loop(0, R, add_stream, 0, unroll=True)
+    lax.fori_loop(0, R, add_stream, 0)
 
     def add_cross(d):
         for e in range(2):

time: 22.6 us -> 22.6 us (level)
  the two profiles are of different devices: /device:TPU:21 before, /device:TPU:17 now
where the time goes in v5:
time: 22.6 us; the launch traced here: 22.2 us
  Pallas kernels  20.6 us (91%)
  local copies, waits for them, and re-layouts  0.97 us (4%)
  between operations  0.66 us (3%)
    pallas_call x1, Pallas kernels, body(): pl.pallas_call(functools.partial(kernel, ns, nc, R, C), out_shape=pltpu.V...  20.6 us
    unnamed x1, local copies, waits for them, and re-layouts  0.97 us

profile of v5, /device:TPU:17, one launch (start us, length us, event | category | flops | bytes accessed | tf_op | source)
XLA Modules:
  0.0 22.2 jit_solution(15130119428062814399)
XLA Ops:
  0.7 20.6 %shard_map.64 = f32[4,8,64,128]{3,2,1,0:T(8,128)S(1)} custom-call(s32[1,1]{1,0:T(1,128)S(6)} %copy.9.live_ref, bf16[4,8,64,128]{3,2,1,0:T(8,128)(2,1)} %residual.1, bf16[1,96,64,256]{3,2,1,0:T(8,128)(2,1)} %inverse.1, s32[1,4,96]{2,1,0:T(4,128)} %bitcast.1, s32[4,8]{1,0:T(4,128)} %aggregate_in.1, f32[32,32]{1,0:T(8,128)} %coarse_in.1), custom_call_target="tpu_custom_call" | custom-call | flops 402653184 | bytes 4718592 | tf_op jit(solution)/shard_map/pallas_call | solution.py:359
  21.2 1.0 %copy.8 = f32[4,8,64,128]{3,2,1,0:T(8,128)} copy(f32[4,8,64,128]{3,2,1,0:T(8,128)S(1)} %shard_map.64) | data formatting | bytes 2097152

commit v6 on v5

--- a/solution.py
+++ b/solution.py
@@ -29,13 +29,16 @@
 
     far = lax.rem(s, 2)
     near = 1 - far
+    long = lax.rem(c, 2)
+    short = 1 - long
 
     def s_has(d):
         to = s + 2 * d - 1
         return (to >= 0) & (to < ns)
 
     def c_has(e):
-        return c > 0 if e == 0 else c < nc - 1
+        to = c + 2 * e - 1
+        return (to >= 0) & (to < nc)
 
     def s_to(d):
         return {"stream": jnp.clip(s + 2 * d - 1, 0, ns - 1)}
@@ -102,9 +105,15 @@
 
     mask(tuple(range(W)) + tuple(range(C - W, C)))
 
-    own_cols = (pl.ds(W, W), pl.ds(C, W))
-    halo_cols = (pl.ds(C + W, W), pl.ds(0, W))
-    side_cols = (pl.ds(0, W), pl.ds(C + W, W))
+    def own_cols(e):
+        return pl.ds(W + e * (C - W), W)
+
+    def halo_cols(e):
+        return pl.ds((1 - e) * (C + W), W)
+
+    def side_cols(e):
+        return pl.ds(e * (C + W), W)
+
     mid_cols = pl.ds(W, C)
 
     def remote(src, dst, send, recv, to):
@@ -120,7 +129,7 @@
 
     def cross1(e, d):
         i = 2 * e + d
-        return remote(ext4.at[own_rows(d), own_cols[e]], ext4.at[own_rows(d), halo_cols[e]],
+        return remote(ext4.at[own_rows(d), own_cols(e)], ext4.at[own_rows(d), halo_cols(e)],
                       h_send.at[i], h_recv.at[i], c_to(e))
 
     def stream1(d):
@@ -129,7 +138,7 @@
 
     def corner1(d, e):
         i = 2 * e + d
-        return remote(ext4.at[own_rows(d), side_cols[e]], ext4.at[halo_rows(d), side_cols[e]],
+        return remote(ext4.at[own_rows(d), side_cols(e)], ext4.at[halo_rows(d), side_cols(e)],
                       q_send.at[i], q_recv.at[i], s_to(d))
 
     def far_rows(d):
@@ -137,7 +146,7 @@
 
     def corner2(d, e):
         i = 2 * e + d
-        return remote(fix4.at[far_rows(d), side_cols[e]], rs.at[pl.ds(W * (1 - d), W), side_cols[e]],
+        return remote(fix4.at[far_rows(d), side_cols(e)], rs.at[pl.ds(W * (1 - d), W), side_cols(e)],
                       b_send.at[i], b_recv.at[i], s_to(d))
 
     def stream2(d):
@@ -156,11 +165,20 @@
     pl.semaphore_wait(barrier, ns - 1 + c_has(0).astype(jnp.int32) + c_has(1).astype(jnp.int32))
 
     for d in (far, near):
-        for e in range(2):
+        for e in (long, short):
             when(c_has(e), lambda: cross1(e, d).start())
     mask(range(W, C - W))
     for d in (far, near):
         when(s_has(d), lambda: stream1(d).start())
+
+    def forward(d):
+        for e in (short, long):
+            @pl.when(c_has(1 - e))
+            def _():
+                cross1(e, d).wait_recv()
+                when(s_has(d), lambda: corner1(d, 1 - e).start())
+
+    forward(far)
 
     def sums(i, carry):
         for j in range(0, C, 2):
@@ -201,12 +219,7 @@
     for k in range(1, ns):
         give(k).start()
 
-    for d in (far, near):
-        for e in range(2):
-            @pl.when(c_has(1 - e))
-            def _():
-                cross1(e, d).wait_recv()
-                when(s_has(d), lambda: corner1(d, 1 - e).start())
+    forward(near)
 
     loads[3].wait()
     loads[4].wait()
@@ -232,7 +245,7 @@
             fix4[i, j] = fix_of(i, j).astype(bf16)
 
     def fold(d):
-        for e in range(2):
+        for e in (long, short):
             @pl.when(c_has(e))
             def _():
                 when(s_has(d), lambda: corner2(1 - d, e).wait_recv())
@@ -257,72 +270,65 @@
         for k in range(1, ns):
             share(k, s).start()
 
+    def sweep(first, count, cols):
+        def row(u, carry):
+            put(first + u, cols)
+            return carry
+
+        lax.fori_loop(0, count, row, 0)
+
     def edges(p, carry):
-        d = lax.rem(p, 2) * far + (1 - lax.rem(p, 2)) * near
-        first = jnp.where(p < 2, d * (R + W), W + W * d)
+        d = jnp.where(p == 0, near, far)
         for u in range(W):
-            put(first + u, edge)
-
-        @pl.when(p < 2)
-        def _():
-            for e in range(2):
-                when(s_has(d) & c_has(e), lambda: corner2(d, e).start())
-
-        @pl.when(p == 2)
-        def _():
-            fold(near)
-            coarse_step()
-
+            put(d * (R + W) + u, edge)
+        for e in range(2):
+            when(s_has(d) & c_has(e), lambda: corner2(d, e).start())
         return carry
 
-    lax.fori_loop(0, 4, edges, 0)
-
-    def rows(p, carry):
-        q = p // W
-        d = jnp.where(q == 0, far, near)
-        put(jnp.where(q < 2, d * (R + W) + lax.rem(p, W), p - W), middle)
-
-        @pl.when((lax.rem(p, W) == W - 1) & (q < 2))
-        def _():
-            when(s_has(d), lambda: stream2(d).start())
-            when(q == 0, lambda: fold(far))
-
-        return carry
-
-    lax.fori_loop(0, 2 * W + R, rows, 0)
+    lax.fori_loop(0, 2, edges, 0)
+    sweep(W + W * near, W, edge)
+    fold(near)
+    sweep(far * (R + W), W, middle)
+    when(s_has(far), lambda: stream2(far).start())
+    sweep(W + W * far, W, edge)
+    fold(far)
+    coarse_step()
+    sweep(near * (R + W), W, middle)
+    when(s_has(near), lambda: stream2(near).start())
+    sweep(W, R, middle)
 
     for k in range(1, ns):
         share(k, lax.rem(s + ns - k, ns)).wait_recv()
-
-    for d in range(2):
-        when(s_has(1 - d), lambda: stream2(d).wait_recv())
 
     def kept(i, j, value):
         keep = jnp.full(value.shape, i * C + j, jnp.int32) < live
         return jnp.where(keep, value, 0.0)
 
-    def add_stream(i, carry):
-        for j in range(C):
-            values = coarse_all[aggregate[i, j]]
-            spread = jnp.concatenate(
-                [jnp.broadcast_to(values[f:f + 1], (width // 4, sides)) for f in range(4)], axis=0)
-            fine = fix4[i + W, j + W].astype(f32) + rs[i, j + W].astype(f32)
-            out[i, j] = kept(i, j, fine + spread)
-        return carry
-
-    lax.fori_loop(0, R, add_stream, 0)
-
-    def add_cross(d):
-        for e in range(2):
+    def finish(d):
+        when(s_has(d), lambda: stream2(1 - d).wait_recv())
+
+        def add_stream(u, carry):
+            i = W * d + u
+            for j in range(C):
+                values = coarse_all[aggregate[i, j]]
+                spread = jnp.concatenate(
+                    [jnp.broadcast_to(values[f:f + 1], (width // 4, sides)) for f in range(4)],
+                    axis=0)
+                fine = fix4[i + W, j + W].astype(f32) + rs[i, j + W].astype(f32)
+                out[i, j] = kept(i, j, fine + spread)
+            return carry
+
+        lax.fori_loop(0, W, add_stream, 0)
+        for e in (short, long):
             when(c_has(1 - e), lambda: cross2(e, d).wait_recv())
-        for t in range(W):
-            i = W * d + t
+        for u in range(W):
+            i = W * d + u
             for j in range(W):
                 for col, at in ((j, j), (C - W + j, W + j)):
                     out[i, col] = kept(i, col, out[i, col] + rc[i, at].astype(f32))
 
-    add_cross(near)
-    add_cross(far)
+    finish(near)
+    finish(far)
 
     for e in range(2):
         @pl.when(c_has(e))

time: 22.6 us -> 22.1 us (0.978); the launches traced: 22.2 us -> 22 us
  no operation moved by 1% of the time
where the time goes in v6:
time: 22.1 us; the launch traced here: 22 us
  Pallas kernels  20.4 us (92%)
  local copies, waits for them, and re-layouts  0.97 us (4%)
  between operations  0.66 us (3%)
    pallas_call x1, Pallas kernels, body(): pl.pallas_call(functools.partial(kernel, ns, nc, R, C), out_shape=pltpu.V...  20.4 us
    unnamed x1, local copies, waits for them, and re-layouts  0.97 us

profile of v6, /device:TPU:17, one launch (start us, length us, event | category | flops | bytes accessed | tf_op | source)
XLA Modules:
  0.0 22.0 jit_solution(14531507628459325075)
XLA Ops:
  0.7 20.4 %shard_map.64 = f32[4,8,64,128]{3,2,1,0:T(8,128)S(1)} custom-call(s32[1,1]{1,0:T(1,128)S(6)} %copy.9.live_ref, bf16[4,8,64,128]{3,2,1,0:T(8,128)(2,1)} %residual.1, bf16[1,96,64,256]{3,2,1,0:T(8,128)(2,1)} %inverse.1, s32[1,4,96]{2,1,0:T(4,128)} %bitcast.1, s32[4,8]{1,0:T(4,128)} %aggregate_in.1, f32[32,32]{1,0:T(8,128)} %coarse_in.1), custom_call_target="tpu_custom_call" | custom-call | flops 402653184 | bytes 4718592 | tf_op jit(solution)/shard_map/pallas_call | solution.py:365
  21.0 1.0 %copy.8 = f32[4,8,64,128]{3,2,1,0:T(8,128)} copy(f32[4,8,64,128]{3,2,1,0:T(8,128)S(1)} %shard_map.64) | data formatting | bytes 2097152

commit v7 on v6

--- a/solution.py
+++ b/solution.py
@@ -53,8 +53,7 @@
         pltpu.make_async_copy(pattern_in, pattern, in_sem.at[3]),
         pltpu.make_async_copy(inverse.at[0], a_mat, in_sem.at[4]),
     ]
-    for load in loads:
-        load.start()
+    loads[0].start()
 
     barrier = pltpu.get_barrier_semaphore()
     for e in range(2):
@@ -65,6 +64,9 @@
     for k in range(1, ns):
         pl.semaphore_signal(barrier, inc=1, device_id={"stream": lax.rem(s + k, ns)},
                             device_id_type=pl.DeviceIdType.MESH)
+
+    for load in loads[1:]:
+        load.start()
 
     def zero(ref, rows, cols):
         ref[rows[0]:rows[1], cols[0]:cols[1]] = jnp.zeros(
@@ -277,20 +279,23 @@
 
         lax.fori_loop(0, count, row, 0)
 
-    def edges(p, carry):
-        d = jnp.where(p == 0, near, far)
+    def margin(d):
         for u in range(W):
             put(d * (R + W) + u, edge)
-        for e in range(2):
+        for e in (long, short):
             when(s_has(d) & c_has(e), lambda: corner2(d, e).start())
-        return carry
-
-    lax.fori_loop(0, 2, edges, 0)
-    sweep(W + W * near, W, edge)
+
+    def own_edges(d):
+        for u in range(W):
+            put(W + W * d + u, edge)
+
+    margin(near)
+    own_edges(near)
+    margin(far)
     fold(near)
     sweep(far * (R + W), W, middle)
     when(s_has(far), lambda: stream2(far).start())
-    sweep(W + W * far, W, edge)
+    own_edges(far)
     fold(far)
     coarse_step()
     sweep(near * (R + W), W, middle)

time: 22.1 us -> 22 us (level)
  no operation moved by 1% of the time
where the time goes in v7:
time: 22 us; the launch traced here: 21.8 us
  Pallas kernels  20.2 us (92%)
  local copies, waits for them, and re-layouts  0.97 us (4%)
  between operations  0.66 us (3%)
    pallas_call x1, Pallas kernels, body(): pl.pallas_call(functools.partial(kernel, ns, nc, R, C), out_shape=pltpu.V...  20.2 us
    unnamed x1, local copies, waits for them, and re-layouts  0.97 us

profile of v7, /device:TPU:17, one launch (start us, length us, event | category | flops | bytes accessed | tf_op | source)
XLA Modules:
  0.0 21.8 jit_solution(14689864755543620703)
XLA Ops:
  0.7 20.2 %shard_map.64 = f32[4,8,64,128]{3,2,1,0:T(8,128)S(1)} custom-call(s32[1,1]{1,0:T(1,128)S(6)} %copy.9.live_ref, bf16[4,8,64,128]{3,2,1,0:T(8,128)(2,1)} %residual.1, bf16[1,96,64,256]{3,2,1,0:T(8,128)(2,1)} %inverse.1, s32[1,4,96]{2,1,0:T(4,128)} %bitcast.1, s32[4,8]{1,0:T(4,128)} %aggregate_in.1, f32[32,32]{1,0:T(8,128)} %coarse_in.1), custom_call_target="tpu_custom_call" | custom-call | flops 402653184 | bytes 4718592 | tf_op jit(solution)/shard_map/pallas_call | solution.py:370
  20.9 1.0 %copy.8 = f32[4,8,64,128]{3,2,1,0:T(8,128)} copy(f32[4,8,64,128]{3,2,1,0:T(8,128)S(1)} %shard_map.64) | data formatting | bytes 2097152

commit v8 on v7

--- a/solution.py
+++ b/solution.py
@@ -356,6 +356,18 @@
         share(k, s).wait_send()
 
 
+def flush(held, out, sem):
+    half = held.shape[1] // 2
+    copies = [
+        pltpu.make_async_copy(held.at[i, pl.ds(h * half, half)], out.at[i, pl.ds(h * half, half)],
+                              sem.at[2 * i + h])
+        for i in range(held.shape[0]) for h in range(2)]
+    for copy in copies:
+        copy.start()
+    for copy in copies:
+        copy.wait()
+
+
 def body(ns, nc, residual, approx_inverse, pattern, live_blocks, block_aggregate, coarse_inverse):
     R, C, width, sides = residual.shape
     _, extent, _, depth = approx_inverse.shape
@@ -367,7 +379,7 @@
     RE, CE = R + 2 * W, C + 2 * W
     links = jnp.transpose(pattern, (0, 2, 1))
     operands = (residual, approx_inverse, links, block_aggregate, coarse_inverse)
-    return pl.pallas_call(
+    held = pl.pallas_call(
         functools.partial(kernel, ns, nc, R, C),
         out_shape=pltpu.VMEM(residual.shape, f32),
         in_specs=[pl.BlockSpec(memory_space=pltpu.SMEM)] + [hbm] * 5,
@@ -399,6 +411,14 @@
             bytes_accessed=extent * width * depth * 2 + residual.size * 6,
             transcendentals=0),
     )(live_blocks, *(pltpu.with_memory_space_constraint(array, pltpu.HBM) for array in operands))
+    return pl.pallas_call(
+        flush,
+        out_shape=jax.ShapeDtypeStruct(residual.shape, f32),
+        in_specs=[vmem],
+        out_specs=hbm,
+        scratch_shapes=[dma((2 * R,))],
+        cost_estimate=pl.CostEstimate(flops=0, bytes_accessed=residual.size * 4, transcendentals=0),
+    )(held)
 
 
 def solution(mesh):

time: 22 us -> 24.2 us (1.100)
  Pallas kernels: 20.2 us -> 22.4 us
    pallas_call x0 -> x1, Pallas kernels: none -> 2.25 us  [body(): pl.pallas_call(flush, out_shape=jax.ShapeDtypeStruct(residual.shape, f32)...]
    unnamed x1 -> x2, local copies, waits for them, and re-layouts: 0.97 us -> 0.98 us
where the time goes in v8:
time: 24.2 us; the launch traced here: 24.1 us
  Pallas kernels  22.4 us (93%)
  local copies, waits for them, and re-layouts  0.98 us (4%)
  between operations  0.67 us (3%)
    pallas_call x1, Pallas kernels, body(): pl.pallas_call(functools.partial(kernel, ns, nc, R, C), out_shape=pltpu.V...  20.2 us
    pallas_call x1, Pallas kernels, body(): pl.pallas_call(flush, out_shape=jax.ShapeDtypeStruct(residual.shape, f32)...  2.25 us
    unnamed x2, local copies, waits for them, and re-layouts  0.98 us

profile of v8, /device:TPU:17, one launch (start us, length us, event | category | flops | bytes accessed | tf_op | source)
XLA Modules:
  0.0 24.1 jit_solution(9769378720468449862)
XLA Ops:
  0.7 20.2 %shard_map.64.held = f32[4,8,64,128]{3,2,1,0:T(8,128)S(1)} custom-call(s32[1,1]{1,0:T(1,128)S(6)} %copy.7.live_ref, bf16[4,8,64,128]{3,2,1,0:T(8,128)(2,1)} %residual.1, bf16[1,96,64,256]{3,2,1,0:T(8,128)(2,1)} %inverse.1, s32[1,4,96]{2,1,0:T(4,128)} %bitcast.1, s32[4,8]{1,0:T(4,128)} %aggregate_in.1, f32[32,32]{1,0:T(8,128)} %coarse_in.1), custom_call_target="tpu_custom_call" | custom-call | flops 402653184 | bytes 4718592 | tf_op jit(solution)/shard_map/pallas_call | solution.py:382
  20.9 0.0 copy-start
  20.9 1.0 %copy-done = f32[4,8,64,128]{3,2,1,0:T(8,128)} copy-done((f32[4,8,64,128]{3,2,1,0:T(8,128)}, f32[4,8,64,128]{3,2,1,0:T(8,128)S(1)}, u32[]{:S(2)}) %copy-start) | copy-done | bytes 1048600
  21.8 2.2 %shard_map.65 = f32[4,8,64,128]{3,2,1,0:T(8,128)} custom-call(f32[4,8,64,128]{3,2,1,0:T(8,128)} %copy-done), custom_call_target="tpu_custom_call" | custom-call | bytes 1048576 | tf_op jit(solution)/shard_map/pallas_call | solution.py:414
Async XLA Ops:
  20.9 1.0 %copy-start = (f32[4,8,64,128]{3,2,1,0:T(8,128)}, f32[4,8,64,128]{3,2,1,0:T(8,128)S(1)}, u32[]{:S(2)}) copy-start(f32[4,8,64,128]{3,2,1,0:T(8,128)S(1)} %shard_map.64.held) | copy-start | bytes 3145732

commit v9 on v7

--- a/solution.py
+++ b/solution.py
@@ -46,14 +46,19 @@
     def c_to(e):
         return {"cross": jnp.clip(c + 2 * e - 1, 0, nc - 1)}
 
+    parts = (pl.ds(0, W), pl.ds(C - W, W), pl.ds(W, C - 2 * W))
+    first = [
+        pltpu.make_async_copy(residual.at[:, part], res.at[:, part], in_sem.at[5 + n])
+        for n, part in enumerate(parts)]
     loads = [
-        pltpu.make_async_copy(residual, res, in_sem.at[0]),
+        None,
         pltpu.make_async_copy(aggregate_in, aggregate, in_sem.at[1]),
         pltpu.make_async_copy(coarse_in, coarse_inv, in_sem.at[2]),
         pltpu.make_async_copy(pattern_in, pattern, in_sem.at[3]),
         pltpu.make_async_copy(inverse.at[0], a_mat, in_sem.at[4]),
     ]
-    loads[0].start()
+    for load in first:
+        load.start()
 
     barrier = pltpu.get_barrier_semaphore()
     for e in range(2):
@@ -93,7 +98,8 @@
         zero(rc, (0, R), (W, 2 * W))
 
     live = live_ref[0, 0]
-    loads[0].wait()
+    first[0].wait()
+    first[1].wait()
 
     def mask(cols):
         def row(i, carry):
@@ -169,6 +175,7 @@
     for d in (far, near):
         for e in (long, short):
             when(c_has(e), lambda: cross1(e, d).start())
+    first[2].wait()
     mask(range(W, C - W))
     for d in (far, near):
         when(s_has(d), lambda: stream1(d).start())
@@ -387,7 +394,7 @@
             pltpu.VMEM((ns, 4 * owned, sides), f32),
             pltpu.VMEM((ns - 1, 4 * owned, sides), f32),
             pltpu.VMEM((ns * owned, 4, sides), f32),
-            dma((5,)),
+            dma((8,)),
             dma((4,)), dma((4,)), dma((2,)), dma((2,)), dma((4,)), dma((4,)),
             dma((ns - 1,)), dma((ns - 1,)), dma((ns - 1,)), dma((ns - 1,)),
             dma((4,)), dma((4,)), dma((2,)), dma((2,)), dma((4,)), dma((4,)),

time: 22 us -> 22 us (level)
  no operation moved by 1% of the time
where the time goes in v9:
time: 22 us; the launch traced here: 21.9 us
  Pallas kernels  20.2 us (92%)
  local copies, waits for them, and re-layouts  0.97 us (4%)
  between operations  0.66 us (3%)
    pallas_call x1, Pallas kernels, body(): pl.pallas_call(functools.partial(kernel, ns, nc, R, C), out_shape=pltpu.V...  20.2 us
    unnamed x1, local copies, waits for them, and re-layouts  0.97 us

profile of v9, /device:TPU:17, one launch (start us, length us, event | category | flops | bytes accessed | tf_op | source)
XLA Modules:
  0.0 21.9 jit_solution(13876244658538470283)
XLA Ops:
  0.7 20.2 %shard_map.64 = f32[4,8,64,128]{3,2,1,0:T(8,128)S(1)} custom-call(s32[1,1]{1,0:T(1,128)S(6)} %copy.9.live_ref, bf16[4,8,64,128]{3,2,1,0:T(8,128)(2,1)} %residual.1, bf16[1,96,64,256]{3,2,1,0:T(8,128)(2,1)} %inverse.1, s32[1,4,96]{2,1,0:T(4,128)} %bitcast.1, s32[4,8]{1,0:T(4,128)} %aggregate_in.1, f32[32,32]{1,0:T(8,128)} %coarse_in.1), custom_call_target="tpu_custom_call" | custom-call | flops 402653184 | bytes 4718592 | tf_op jit(solution)/shard_map/pallas_call | solution.py:377
  20.9 1.0 %copy.8 = f32[4,8,64,128]{3,2,1,0:T(8,128)} copy(f32[4,8,64,128]{3,2,1,0:T(8,128)S(1)} %shard_map.64) | data formatting | bytes 2097152
